TPU v7x, 32 devices: a whole 2x2x4 slice. The times are simulated.
32 devices in a mesh: dp: 8 (over z, y), expert: 4 (over x, core).
Axes of the slice: x: 2, y: 2, z: 4, core: 2. Of those that a mesh axis runs over, the one named last changes fastest.
Arguments:
- tokens: bfloat16 [16384, 768], P(('dp', 'expert')), may hold values from -6 to 6
- segment_ids: int32 [32, 512], P(('dp', 'expert')), may hold values from 0 to 5, never falling along the last dimension, each value on 1 to 256 neighbouring positions
- expert_ids: int32 [16384, 2], P(('dp', 'expert')), may hold values from 0 to 7, all different within a row
- upstream: bfloat16 [16384, 768], P(('dp', 'expert')), may hold values from -6 to 6
- norm_first: bfloat16 [768], P(('dp', 'expert')), may hold values from 0.5 to 1.5
- qkv_weight: bfloat16 [768, 2304], P(('dp', 'expert')), may hold values from -0.21875 to 0.21875
- out_weight: bfloat16 [768, 768], P(('dp', 'expert')), may hold values from -0.625 to 0.625
- norm_second: bfloat16 [768], P(('dp', 'expert')), may hold values from 0.5 to 1.5
- router_weight: bfloat16 [768, 8], P(('dp', 'expert')), may hold values from -0.15625 to 0.15625
- shared_gate_up: bfloat16 [768, 4096], P(('dp', 'expert')), may hold values from -0.21875 to 0.21875
- shared_down: bfloat16 [2048, 768], P(('dp', 'expert')), may hold values from -0.1875 to 0.1875
- expert_gate_up: bfloat16 [8, 768, 4096], P('expert', 'dp'), may hold values from -0.21875 to 0.21875
- expert_down: bfloat16 [8, 2048, 768], P('expert', 'dp'), may hold values from -0.1875 to 0.1875
Outputs:
- mixed: bfloat16 [16384, 768], P(('dp', 'expert'))
- input_grad: float32 [16384, 768], P(('dp', 'expert'))
- norm_first_grad: float32 [768], P(('dp', 'expert'))
- qkv_grad: float32 [768, 2304], P(('dp', 'expert'))
- out_weight_grad: float32 [768, 768], P(('dp', 'expert'))
- norm_second_grad: float32 [768], P(('dp', 'expert'))
- router_grad: float32 [768, 8], P(('dp', 'expert'))
- shared_gate_up_grad: float32 [768, 4096], P(('dp', 'expert'))
- shared_down_grad: float32 [2048, 768], P(('dp', 'expert'))
- expert_gate_up_grad: float32 [8, 768, 4096], P('expert', 'dp')
- expert_down_grad: float32 [8, 2048, 768], P('expert', 'dp')
Inputs may be any that keep to these rules, and one draw needn't show every extreme that they name: `expert_ids`: each token names two different experts. `segment_ids`: segment numbers never fall along a sequence, and each of the 6 numbers appears in every sequence.
All inputs are finite; a program needn't handle non-finite values.
Results may differ from a plain program's by a relative error of at most 0.015.
Values may be sent and summed in bfloat16 or wider, within the bound.
No kernel may reach another device: no remote copies, remote signals or barrier semaphores. Data moves between devices by JAX's collectives and lax.ppermute only.
A program may use at most 256 MiB of HBM per device.

v0:
```python
import jax
import jax.numpy as jnp
from jax import lax
from jax.sharding import PartitionSpec as P

D = 768
HEADS = 12
HEAD_DIM = 64
FF = 2048
FS = 2048


epsilon = 1e-06


def rope_tables(length, head_width):
    half_width = head_width // 2
    frequency = 10000.0 ** (-jnp.arange(half_width, dtype=jnp.float32) / half_width)
    angles = jnp.arange(length, dtype=jnp.float32)[:, None] * frequency[None, :]
    angles = jnp.concatenate([angles, angles], axis=-1)[:, None, :]
    return (jnp.cos(angles), jnp.sin(angles))


def rotate(values, cosine_table, sine_table):
    half_width = values.shape[-1] // 2
    turned = jnp.concatenate([-values[..., half_width:], values[..., :half_width]], axis=-1)
    return values * cosine_table + turned * sine_table


def rotate_back(grads, cosine_table, sine_table):
    half_width = grads.shape[-1] // 2
    sined = grads * sine_table
    return grads * cosine_table + jnp.concatenate(
        [sined[..., half_width:], -sined[..., :half_width]], axis=-1
    )


def silu_parts(pre):
    sigmoid = jax.nn.sigmoid(pre)
    return (pre * sigmoid, sigmoid * (1.0 + pre * (1.0 - sigmoid)))


def slot_table(expert_ids, experts, capacity):
    flat_ids = expert_ids.reshape(-1)
    one_hot = (flat_ids[:, None] == jnp.arange(experts, dtype=jnp.int32)[None, :]).astype(jnp.int32)
    earlier = jnp.cumsum(one_hot, axis=0) - one_hot
    slot_rank = jnp.sum(earlier * one_hot, axis=1).reshape(expert_ids.shape)
    kept_mask = slot_rank < capacity
    slot_index = jnp.where(kept_mask, expert_ids * capacity + slot_rank, experts * capacity)
    return (kept_mask, slot_index)


def norm_back(grad_normed, normed, scale):
    return scale * (grad_normed - normed * jnp.mean(grad_normed * normed, axis=-1, keepdims=True))


def body(
    tokens,
    segment_ids,
    expert_ids,
    upstream,
    norm_first,
    qkv_weight,
    out_weight,
    norm_second,
    router_weight,
    shared_gate_up,
    shared_down,
    expert_gate_up,
    expert_down,
):
    length = tokens.shape[0]
    experts = expert_gate_up.shape[0] * lax.axis_size("expert")
    capacity = length * 2 // experts
    score_scale = HEAD_DIM ** (-0.5)
    dense_full = (
        lax.all_gather(norm_first, ("dp", "expert"), axis=0, tiled=True),
        lax.all_gather(norm_second, ("dp", "expert"), axis=0, tiled=True),
        lax.all_gather(qkv_weight, ("dp", "expert"), axis=0, tiled=True),
        lax.all_gather(out_weight, ("dp", "expert"), axis=0, tiled=True),
        lax.all_gather(router_weight, ("dp", "expert"), axis=0, tiled=True),
        lax.all_gather(shared_gate_up, ("dp", "expert"), axis=0, tiled=True),
        lax.all_gather(shared_down, ("dp", "expert"), axis=0, tiled=True),
    )
    expert_full = (
        lax.all_gather(expert_gate_up, "dp", axis=1, tiled=True),
        lax.all_gather(expert_down, "dp", axis=1, tiled=True),
    )
    gain_one = dense_full[0].astype(jnp.float32)
    gain_two = dense_full[1].astype(jnp.float32)
    stream = tokens.astype(jnp.float32)
    scale_one = lax.rsqrt(jnp.mean(stream * stream, axis=-1, keepdims=True) + epsilon)
    normed_one = stream * scale_one
    normed_low = (normed_one * gain_one).astype(jnp.bfloat16)
    projected = jnp.dot(normed_low, dense_full[2], preferred_element_type=jnp.float32)
    cosine_table, sine_table = rope_tables(length, HEAD_DIM)
    query_rot = rotate(
        projected[:, :D].reshape(length, HEADS, HEAD_DIM), cosine_table, sine_table
    ).astype(jnp.bfloat16)
    key_rot = rotate(
        projected[:, D : 2 * D].reshape(length, HEADS, HEAD_DIM), cosine_table, sine_table
    ).astype(jnp.bfloat16)
    value_low = projected[:, 2 * D :].astype(jnp.bfloat16).reshape(length, HEADS, HEAD_DIM)
    query_heads = jnp.swapaxes(query_rot, 0, 1)
    key_heads = jnp.swapaxes(key_rot, 0, 1)
    value_heads = jnp.swapaxes(value_low, 0, 1)
    position = jnp.arange(length)
    segments = segment_ids[0]
    allowed = (position[:, None] >= position[None, :]) & (segments[:, None] == segments[None, :])

    def head_scores(query_head, key_head):
        scores = (
            jnp.einsum("qd,kd->qk", query_head, key_head, preferred_element_type=jnp.float32)
            * score_scale
        )
        return jnp.where(allowed, scores, -1000000000.0)

    def head_forward(parts):
        query_head, key_head, value_head = parts
        scores = head_scores(query_head, key_head)
        top_score = jnp.max(scores, axis=-1, keepdims=True)
        exp_scores = jnp.exp(scores - top_score)
        row_total = jnp.sum(exp_scores, axis=-1, keepdims=True)
        attn_probs = exp_scores / row_total
        head_out = jnp.einsum(
            "qk,kd->qd",
            attn_probs.astype(jnp.bfloat16),
            value_head,
            preferred_element_type=jnp.float32,
        )
        return (head_out, (top_score + jnp.log(row_total))[:, 0])

    def head_backward(parts):
        query_head, key_head, value_head, grad_head, log_total = parts
        scores = head_scores(query_head, key_head)
        attn_probs = jnp.exp(scores - log_total[:, None])
        grad_value = jnp.einsum(
            "qk,qd->kd",
            attn_probs.astype(jnp.bfloat16),
            grad_head,
            preferred_element_type=jnp.float32,
        )
        grad_probs = jnp.einsum(
            "qd,kd->qk", grad_head, value_head, preferred_element_type=jnp.float32
        )
        grad_scores = attn_probs * (
            grad_probs - jnp.sum(grad_probs * attn_probs, axis=-1, keepdims=True)
        )
        grad_low = grad_scores.astype(jnp.bfloat16)
        grad_query = (
            jnp.einsum("qk,kd->qd", grad_low, key_head, preferred_element_type=jnp.float32)
            * score_scale
        )
        grad_key = (
            jnp.einsum("qk,qd->kd", grad_low, query_head, preferred_element_type=jnp.float32)
            * score_scale
        )
        return (grad_query, grad_key, grad_value)

    head_outs, log_totals = lax.map(head_forward, (query_heads, key_heads, value_heads))
    attended = jnp.swapaxes(head_outs, 0, 1).reshape(length, D).astype(jnp.bfloat16)
    stream_mid = stream + jnp.dot(attended, dense_full[3], preferred_element_type=jnp.float32)
    scale_two = lax.rsqrt(jnp.mean(stream_mid * stream_mid, axis=-1, keepdims=True) + epsilon)
    normed_two = stream_mid * scale_two
    expert_in = (normed_two * gain_two).astype(jnp.bfloat16)
    logits = jnp.dot(expert_in, dense_full[4], preferred_element_type=jnp.float32)
    picker = (expert_ids[:, :, None] == jnp.arange(experts, dtype=jnp.int32)[None, None, :]).astype(
        jnp.float32
    )
    chosen = jnp.sum(picker * logits[:, None, :], axis=-1)
    chosen_top = jnp.max(chosen, axis=1, keepdims=True)
    chosen_exp = jnp.exp(chosen - chosen_top)
    gate_values = chosen_exp / jnp.sum(chosen_exp, axis=1, keepdims=True)
    kept_mask, slot_index = slot_table(expert_ids, experts, capacity)
    kept_float = kept_mask.astype(jnp.float32)
    mix_weight = kept_float * gate_values
    shared_pre = jnp.dot(expert_in, dense_full[5], preferred_element_type=jnp.float32)
    shared_act, shared_slope = silu_parts(shared_pre[:, :FS])
    shared_up = shared_pre[:, FS:]
    shared_hidden = (shared_act * shared_up).astype(jnp.bfloat16)
    shared_out = jnp.dot(shared_hidden, dense_full[6], preferred_element_type=jnp.float32)
    flat_index = slot_index.reshape(-1)
    repeated = jnp.broadcast_to(expert_in[:, None, :], (length, 2, D)).reshape(length * 2, D)
    dispatched = jnp.zeros((experts * capacity + 1, D), jnp.bfloat16).at[flat_index].set(repeated)
    dispatched = dispatched[: experts * capacity].reshape(experts, capacity, D)
    arrived = lax.all_to_all(dispatched, "expert", split_axis=0, concat_axis=1, tiled=True)
    expert_pre = jnp.einsum(
        "erd,edf->erf", arrived, expert_full[0], preferred_element_type=jnp.float32
    )
    expert_act, expert_slope = silu_parts(expert_pre[..., :FF])
    expert_up = expert_pre[..., FF:]
    expert_hidden = (expert_act * expert_up).astype(jnp.bfloat16)
    expert_out = jnp.einsum(
        "erf,efd->erd", expert_hidden, expert_full[1], preferred_element_type=jnp.float32
    ).astype(jnp.bfloat16)
    returned = lax.all_to_all(expert_out, "expert", split_axis=1, concat_axis=0, tiled=True)
    returned_rows = jnp.concatenate(
        [returned.reshape(experts * capacity, D), jnp.zeros((1, D), jnp.bfloat16)], axis=0
    )
    picked = returned_rows[slot_index].astype(jnp.float32)
    routed = jnp.sum(mix_weight[:, :, None] * picked, axis=1)
    mixed = (stream_mid + routed + shared_out).astype(jnp.bfloat16)
    dense_back = (
        lax.all_gather(norm_first, ("dp", "expert"), axis=0, tiled=True),
        lax.all_gather(norm_second, ("dp", "expert"), axis=0, tiled=True),
        lax.all_gather(qkv_weight, ("dp", "expert"), axis=0, tiled=True),
        lax.all_gather(out_weight, ("dp", "expert"), axis=0, tiled=True),
        lax.all_gather(router_weight, ("dp", "expert"), axis=0, tiled=True),
        lax.all_gather(shared_gate_up, ("dp", "expert"), axis=0, tiled=True),
        lax.all_gather(shared_down, ("dp", "expert"), axis=0, tiled=True),
    )
    expert_back = (
        lax.all_gather(expert_gate_up, "dp", axis=1, tiled=True),
        lax.all_gather(expert_down, "dp", axis=1, tiled=True),
    )
    cotangent = upstream.astype(jnp.float32)
    shared_down_grad = jnp.einsum(
        "sf,sd->fd", shared_hidden, upstream, preferred_element_type=jnp.float32
    )
    grad_shared_hidden = jnp.einsum(
        "sd,fd->sf", upstream, dense_back[6], preferred_element_type=jnp.float32
    )
    grad_shared_pre = jnp.concatenate(
        [grad_shared_hidden * shared_up * shared_slope, grad_shared_hidden * shared_act], axis=-1
    ).astype(jnp.bfloat16)
    shared_gate_up_grad = jnp.einsum(
        "sd,sf->df", expert_in, grad_shared_pre, preferred_element_type=jnp.float32
    )
    grad_expert_in = jnp.einsum(
        "sf,df->sd", grad_shared_pre, dense_back[5], preferred_element_type=jnp.float32
    )
    grad_gate = kept_float * jnp.sum(cotangent[:, None, :] * picked, axis=-1)
    grad_chosen = gate_values * (
        grad_gate - jnp.sum(gate_values * grad_gate, axis=1, keepdims=True)
    )
    grad_logits = jnp.sum(picker * grad_chosen[:, :, None], axis=1).astype(jnp.bfloat16)
    router_grad = jnp.einsum(
        "sd,se->de", expert_in, grad_logits, preferred_element_type=jnp.float32
    )
    grad_expert_in = grad_expert_in + jnp.einsum(
        "se,de->sd", grad_logits, dense_back[4], preferred_element_type=jnp.float32
    )
    grad_picked = (mix_weight[:, :, None] * cotangent[:, None, :]).reshape(length * 2, D)
    grad_out = jnp.zeros((experts * capacity + 1, D), jnp.float32).at[flat_index].add(grad_picked)
    grad_out = grad_out[: experts * capacity].astype(jnp.bfloat16).reshape(experts, capacity, D)
    grad_made = lax.all_to_all(grad_out, "expert", split_axis=0, concat_axis=1, tiled=True)
    expert_down_grad = jnp.einsum(
        "erf,erd->efd", expert_hidden, grad_made, preferred_element_type=jnp.float32
    )
    grad_hidden = jnp.einsum(
        "erd,efd->erf", grad_made, expert_back[1], preferred_element_type=jnp.float32
    )
    grad_expert_pre = jnp.concatenate(
        [grad_hidden * expert_up * expert_slope, grad_hidden * expert_act], axis=-1
    ).astype(jnp.bfloat16)
    expert_gate_up_grad = jnp.einsum(
        "erd,erf->edf", arrived, grad_expert_pre, preferred_element_type=jnp.float32
    )
    grad_arrived = jnp.einsum(
        "erf,edf->erd", grad_expert_pre, expert_back[0], preferred_element_type=jnp.float32
    ).astype(jnp.bfloat16)
    grad_buffer = lax.all_to_all(grad_arrived, "expert", split_axis=1, concat_axis=0, tiled=True)
    buffer_rows = jnp.concatenate(
        [grad_buffer.reshape(experts * capacity, D), jnp.zeros((1, D), jnp.bfloat16)], axis=0
    )
    grad_expert_in = grad_expert_in + jnp.sum(buffer_rows[slot_index].astype(jnp.float32), axis=1)
    back_gain_one = dense_back[0].astype(jnp.float32)
    back_gain_two = dense_back[1].astype(jnp.float32)
    norm_second_grad = jnp.sum(grad_expert_in * normed_two, axis=0)
    grad_mid = cotangent + norm_back(grad_expert_in * back_gain_two, normed_two, scale_two)
    grad_mid_low = grad_mid.astype(jnp.bfloat16)
    out_weight_grad = jnp.einsum(
        "sd,se->de", attended, grad_mid_low, preferred_element_type=jnp.float32
    )
    grad_attended = jnp.einsum(
        "se,de->sd", grad_mid_low, dense_back[3], preferred_element_type=jnp.float32
    ).astype(jnp.bfloat16)
    grad_heads = jnp.swapaxes(grad_attended.reshape(length, HEADS, HEAD_DIM), 0, 1)
    grad_query, grad_key, grad_value = lax.map(
        head_backward, (query_heads, key_heads, value_heads, grad_heads, log_totals)
    )
    grad_query = rotate_back(jnp.swapaxes(grad_query, 0, 1), cosine_table, sine_table).reshape(
        length, D
    )
    grad_key = rotate_back(jnp.swapaxes(grad_key, 0, 1), cosine_table, sine_table).reshape(
        length, D
    )
    grad_value = jnp.swapaxes(grad_value, 0, 1).reshape(length, D)
    grad_projected = jnp.concatenate([grad_query, grad_key, grad_value], axis=-1).astype(
        jnp.bfloat16
    )
    qkv_grad = jnp.einsum(
        "sd,sf->df", normed_low, grad_projected, preferred_element_type=jnp.float32
    )
    grad_normed = jnp.einsum(
        "sf,df->sd", grad_projected, dense_back[2], preferred_element_type=jnp.float32
    )
    norm_first_grad = jnp.sum(grad_normed * normed_one, axis=0)
    input_grad = grad_mid + norm_back(grad_normed * back_gain_one, normed_one, scale_one)
    dense_sums = (
        lax.psum_scatter(norm_first_grad, ("dp", "expert"), scatter_dimension=0, tiled=True),
        lax.psum_scatter(norm_second_grad, ("dp", "expert"), scatter_dimension=0, tiled=True),
        lax.psum_scatter(qkv_grad, ("dp", "expert"), scatter_dimension=0, tiled=True),
        lax.psum_scatter(out_weight_grad, ("dp", "expert"), scatter_dimension=0, tiled=True),
        lax.psum_scatter(router_grad, ("dp", "expert"), scatter_dimension=0, tiled=True),
        lax.psum_scatter(shared_gate_up_grad, ("dp", "expert"), scatter_dimension=0, tiled=True),
        lax.psum_scatter(shared_down_grad, ("dp", "expert"), scatter_dimension=0, tiled=True),
    )
    final_sums = (
        lax.psum_scatter(
            expert_gate_up_grad.astype(jnp.bfloat16), "dp", scatter_dimension=1, tiled=True
        ).astype(jnp.float32),
        lax.psum_scatter(
            expert_down_grad.astype(jnp.bfloat16), "dp", scatter_dimension=1, tiled=True
        ).astype(jnp.float32),
    )
    return (
        mixed,
        input_grad,
        dense_sums[0],
        dense_sums[2],
        dense_sums[3],
        dense_sums[1],
        dense_sums[4],
        dense_sums[5],
        dense_sums[6],
        final_sums[0],
        final_sums[1],
    )


def solution(mesh):
    in_specs = (
        P(("dp", "expert"), None),
        P(("dp", "expert"), None),
        P(("dp", "expert"), None),
        P(("dp", "expert"), None),
        P(("dp", "expert")),
        P(("dp", "expert"), None),
        P(("dp", "expert"), None),
        P(("dp", "expert")),
        P(("dp", "expert"), None),
        P(("dp", "expert"), None),
        P(("dp", "expert"), None),
        P("expert", "dp", None),
        P("expert", "dp", None),
    )
    out_specs = (
        P(("dp", "expert"), None),
        P(("dp", "expert"), None),
        P(("dp", "expert")),
        P(("dp", "expert"), None),
        P(("dp", "expert"), None),
        P(("dp", "expert")),
        P(("dp", "expert"), None),
        P(("dp", "expert"), None),
        P(("dp", "expert"), None),
        P("expert", "dp", None),
        P("expert", "dp", None),
    )
    return jax.shard_map(body, mesh=mesh, in_specs=in_specs, out_specs=out_specs, check_vma=False)
```

profile of v0, /device:TPU:0, one launch (start us, length us, event | category | flops | bytes accessed | tf_op | source)
XLA Modules:
  0.0 1386.5 jit_solution(13428388380161477134)
XLA Ops:
  11.7 42.1 %all-reduce.8 = (bf16[768]{0:T(1024)(128)(2,1)S(1)}, bf16[768]{0:T(1024)(128)(2,1)S(1)}) all-reduce(bf16[768]{0:T(1024)(128)(2,1)S(1)} %dynamic-update-slice, bf16[768]{0:T(1024)(128)(2,1)S(1)} %dynamic-update-slice.1), channel_id=1, replica_groups=mesh['dp'=8,'expert'=4] {'dp','expert'}, use_global_device_ids=true, to_apply=%add.2 | all-reduce | flops 1536 | bytes 6144
  54.4 40.9 %all-gather = bf16[32,24,8]{1,2,0:T(8,128)(2,1)S(1)} all-gather(bf16[1,24,8]{1,2,0:T(8,128)(2,1)S(1)} %bitcast.243), channel_id=1, replica_groups=mesh['dp'=8,'expert'=4] {'dp','expert'}, dimensions={0}, use_global_device_ids=true | all-gather | bytes 12672 | tf_op jit(solution)/shard_map/all_gather | solution.py:81
  100.9 3.3 mul.356
  104.3 4.3 fusion.85
  122.9 23.4 %while.30 = (s32[]{:T(128)}, bf16[12,512,64]{1,2,0:T(8,128)(2,1)S(1)}, f32[12,512]{1,0:T(8,128)S(1)}, bf16[12,512,64]{2,1,0:T(8,128)(2,1)}, bf16[12,512,64]{2,1,...) while((s32[]{:T(128)}, bf16[12,512,64]{1,2,0:T(8,128)(2,1)S(1)}, ...), condition=%wide.region_4.5_spmd.clone.clone, body=%wide.region_1.4_spmd.clone.sunk.clone | while | flops 69991936 | bytes 3696721 | solution.py:160
  151.2 10.6 scatter_custom_fusion.1
  165.0 4.4 all-to-all-start.2
  172.2 6.2 scatter_custom_fusion
  179.7 9.8 all-to-all-done.2
  189.5 3.6 all-to-all-start
  195.8 17.3 %all-to-all-done = bf16[8,128,768]{2,1,0:T(8,128)(2,1)S(1)} async-done(((bf16[8,128,768]{2,1,0:T(8,128)(2,1)}), bf16[8,128,768]{2,1,0:T(8,128)(2,1)S(1)}, u32[]{:S(2)}, u32[]{:S(2)}) %all-to-all-start) | async-done | bytes 1572896 | tf_op jit(solution)/shard_map/all_to_all | solution.py:186
  214.4 92.9 %all-gather.12.cloned.1.call-done = bf16[2,768,4096]{2,1,0:T(8,128)(2,1)} async-done(((bf16[2,96,4096]{2,1,0:T(8,128)(2,1)}), bf16[2,768,4096]{2,1,0:T(8,128)(2,1)}) %all-gather.12.cloned.1.call-update) | async-done | bytes 12582928 | tf_op jit(solution)/shard_map/all_gather | solution.py:86
  307.3 15.4 %fusion.111 = f32[2,512,4096]{2,1,0:T(8,128)} fusion(bf16[2,512,768]{2,1,0:T(8,128)(2,1)} %bitcast.230, bf16[2,768,4096]{2,1,0:T(8,128)(2,1)} %all-gather.12.cloned.1.call-done), kind=kOutput, calls=%fused_computation.190 | convolution fusion | flops 6442450944 | bytes 30932992 | tf_op jit(solution)/shard_map/erd,edf->erf/dot_general | solution.py:187
  322.7 83.9 %all-gather.14.cloned.1.call-done = bf16[2,2048,768]{2,1,0:T(8,128)(2,1)} async-done(((bf16[2,256,768]{2,1,0:T(8,128)(2,1)}), bf16[2,2048,768]{2,1,0:T(8,128)(2,1)}) %all-gather.14.cloned.1.call-update) | async-done | bytes 6291472 | tf_op jit(solution)/shard_map/all_gather | solution.py:87
  406.6 13.5 multiply_convert_fusion.2
  420.1 8.3 convolution_convert_fusion.1
  429.9 13.1 convolution_convert_fusion
  443.0 34.0 %all-gather.16.cloned.1.call-done = bf16[768,4096]{1,0:T(8,128)(2,1)} async-done(((bf16[24,4096]{1,0:T(8,128)(2,1)}), bf16[768,4096]{1,0:T(8,128)(2,1)}) %all-gather.16.cloned.1.call-update) | async-done | bytes 6291472 | tf_op jit(solution)/shard_map/all_gather | solution.py:82
  477.1 8.5 fusion.112
  485.6 51.7 %all-gather.18.cloned.1.call-done = bf16[2048,768]{1,0:T(8,128)(2,1)} async-done(((bf16[64,768]{1,0:T(8,128)(2,1)}), bf16[2048,768]{1,0:T(8,128)(2,1)}) %all-gather.18.cloned.1.call-update) | async-done | bytes 3145744 | tf_op jit(solution)/shard_map/all_gather | solution.py:83
  537.3 7.5 multiply_convert_fusion.5
  546.1 4.5 fusion.113
  552.3 7.5 convolution_convert_fusion.2
  562.7 3.8 all-to-all-start.1
  566.4 13.9 %fusion.59 = bf16[2,512,768]{2,1,0:T(8,128)(2,1)} fusion(bf16[2,768,4096]{2,1,0:T(8,128)(2,1)} %all-gather.12.cloned.1.call-done, bf16[2,512,2048]{2,1,0:T(8,128)(2,1)} %get-tuple-element.270, bf16[2,512,2048]{2,1,0:T(8,128)(2,1)} %get-tuple-element.269), kind=kOutput, calls=%fused_computation.94 | convolution fusion | flops 6460014592 | bytes 22544384 | tf_op jit(solution)/shard_map/erf,edf->erd/dot_general | solution.py:259
  580.3 4.2 copy.140
  586.5 4.4 all-to-all-start.3
  590.9 8.7 fusion.54
  600.0 5.5 gather_fusion
  605.4 5.0 reshape.371
  610.4 9.5 multiply_reduce_fusion.1
  622.7 5.2 gather_fusion.1
  627.9 5.4 reshape.372
  633.4 6.9 reduce_sum.153
  646.9 8.6 fusion.53
  655.6 3.5 convolution_convert_fusion.3
  661.5 91.6 %while.31 = (s32[]{:T(128)}, f32[12,512,64]{1,2,0:T(8,128)}, f32[12,512,64]{1,2,0:T(8,128)}, bf16[12,512,64]{1,2,0:T(8,128)(2,1)S(1)}, bf16[12,512,64]{2,1,0:T(8...) while((s32[]{:T(128)}, f32[12,512,64]{1,2,0:T(8,128)}, ...), condition=%wide.region_22.23_spmd.clone.clone, body=%wide.region_20.22_spmd.clone.sunk.clone | while | flops 170982912 | bytes 9063529 | solution.py:279
  759.5 5.1 fusion.75
  764.9 6.4 fusion.66
  771.3 39.8 %all-reduce.7 = (f32[768]{0:T(1024)S(1)}, f32[768]{0:T(1024)S(1)}, f32[768,8]{0,1:T(8,128)S(1)}) all-reduce(f32[768]{0:T(1024)S(1)} %get-tuple-element.220, f32[768]{0:T(1024)S(1)} %get-tuple-element.216, f32[768,8]{0,1:T(8,128)S(1)} %fusion.114), channel_id=2, replica_groups=mesh['dp'=8,'expert'=4] {'dp','expert'}, use_global_device_ids=true, to_apply=%region_25.26.clone | all-reduce | flops 7680 | bytes 61440
  812.9 3.8 fusion.65
  816.7 4.7 add_convert_fusion
  823.8 44.5 %reduce-scatter.16.cloned.1.call-done = bf16[2,96,4096]{2,1,0:T(8,128)(2,1)} async-done(((bf16[2,768,4096]{2,1,0:T(8,128)(2,1)}), bf16[2,96,4096]{2,1,0:T(8,128)(2,1)}) %reduce-scatter.16.cloned.1.call-update) | async-done | bytes 1572880 | tf_op jit(solution)/shard_map/reduce_scatter | solution.py:310
  868.3 3.4 convert_element_type.124
  871.8 116.5 %reduce-scatter.14.cloned.1.call-done = f32[64,768]{1,0:T(8,128)} async-done(((f32[2048,768]{1,0:T(8,128)}), f32[64,768]{1,0:T(8,128)}) %reduce-scatter.14.cloned.1.call-update) | async-done | bytes 196624 | tf_op jit(solution)/shard_map/reduce_scatter | solution.py:307
  988.3 104.8 %reduce-scatter.10.cloned.1.call-done = f32[24,768]{1,0:T(8,128)} async-done(((f32[768,768]{1,0:T(8,128)}), f32[24,768]{1,0:T(8,128)}) %reduce-scatter.10.cloned.1.call-update) | async-done | bytes 73744 | tf_op jit(solution)/shard_map/reduce_scatter | solution.py:304
  1093.1 161.0 %reduce-scatter.12.cloned.1.call-done = f32[24,4096]{1,0:T(8,128)} async-done(((f32[768,4096]{1,0:T(8,128)}), f32[24,4096]{1,0:T(8,128)}) %reduce-scatter.12.cloned.1.call-update) | async-done | bytes 393232 | tf_op jit(solution)/shard_map/reduce_scatter | solution.py:306
  1254.1 125.4 %reduce-scatter.8.cloned.1.call-done = f32[24,2304]{1,0:T(8,128)} async-done(((f32[768,2304]{1,0:T(8,128)}), f32[24,2304]{1,0:T(8,128)}) %reduce-scatter.8.cloned.1.call-update) | async-done | bytes 221200 | tf_op jit(solution)/shard_map/reduce_scatter | solution.py:303
  (338 shorter events, 187.0 us)
Async XLA Ops:
  7.2 97.1 %all-gather.8.cloned.1.call-start = ((), (), s32[]{:S(2)}) async-start(), calls=%async_computation.10 | async-start | bytes 3649536 | tf_op jit(solution)/shard_map/all_gather | solution.py:79
  7.9 138.4 %all-gather.10.cloned.1.call-start = ((), (), s32[]{:S(2)}) async-start(), calls=%async_computation.11 | async-start | bytes 1216512 | tf_op jit(solution)/shard_map/all_gather | solution.py:80
  8.7 2.1 copy-start.29
  8.7 298.6 %all-gather.12.cloned.1.call-start = ((), (), s32[]{:S(2)}) async-start(), calls=%async_computation.12 | async-start | bytes 14155776 | tf_op jit(solution)/shard_map/all_gather | solution.py:86
  9.4 1.8 copy-start.36
  9.4 2.1 copy-start.37
  9.4 44.4 %copy-start.14 = (bf16[512,768]{1,0:T(8,128)(2,1)S(1)}, bf16[512,768]{1,0:T(8,128)(2,1)}, u32[]{:S(2)}) copy-start(bf16[512,768]{1,0:T(8,128)(2,1)} %param.17) | copy-start | bytes 2359300
  9.4 397.2 %all-gather.14.cloned.1.call-start = ((), (), s32[]{:S(2)}) async-start(), calls=%async_computation.13 | async-start | bytes 7077888 | tf_op jit(solution)/shard_map/all_gather | solution.py:87
  10.0 467.1 %all-gather.16.cloned.1.call-start = ((), (), s32[]{:S(2)}) async-start(), calls=%async_computation.14 | async-start | bytes 6488064 | tf_op jit(solution)/shard_map/all_gather | solution.py:82
  10.7 43.7 %copy-start.8 = (bf16[12,512,64]{1,2,0:T(8,128)(2,1)}, bf16[12,512,64]{1,2,0:T(8,128)(2,1)S(1)}, u32[]{:S(2)}) copy-start(bf16[12,512,64]{1,2,0:T(8,128)(2,1)S(1)} %fusion.109) | copy-start | bytes 2359300
  11.0 43.4 %copy-start.34 = (bf16[24,8]{0,1:T(8,128)(2,1)S(1)}, bf16[24,8]{0,1:T(8,128)(2,1)}, u32[]{:S(2)}) copy-start(bf16[24,8]{0,1:T(8,128)(2,1)} %param.25) | copy-start | bytes 1156
  53.8 50.4 %copy-start.30 = (f32[768]{0:T(1024)}, f32[768]{0:T(1024)S(1)}, u32[]{:S(2)}) copy-start(f32[768]{0:T(1024)S(1)} %convert_element_type.101) | copy-start | bytes 9220
  54.0 50.2 %copy-start.32 = (f32[512]{0:T(512)}, f32[512]{0:T(512)S(1)}, u32[]{:S(2)}) copy-start(f32[512]{0:T(512)S(1)} %add_rsqrt_fusion.1) | copy-start | bytes 6148
  54.4 59.3 %copy-start.23 = (f32[512,64]{0,1:T(8,128)}, f32[512,64]{0,1:T(8,128)S(1)}, u32[]{:S(2)}) copy-start(f32[512,64]{0,1:T(8,128)S(1)} %get-tuple-element.293) | copy-start | bytes 393220
  54.4 59.3 %copy-start.25 = (f32[512,64]{0,1:T(8,128)}, f32[512,64]{0,1:T(8,128)S(1)}, u32[]{:S(2)}) copy-start(f32[512,64]{0,1:T(8,128)S(1)} %get-tuple-element.294) | copy-start | bytes 393220
  115.8 2.5 copy-start.17
  118.3 1.5 copy-start.13
  121.0 1.9 copy-start.12
  121.0 1.9 copy-start.35
  146.2 3.3 copy-start.7
  146.3 3.3 copy-start.10
  165.0 24.5 %all-to-all-start.2 = ((bf16[8,128,768]{2,1,0:T(8,128)(2,1)}), bf16[8,128,768]{2,1,0:T(8,128)(2,1)}, u32[]{:S(2)}, u32[]{:S(2)}) async-start(bf16[8,128,768]{2,1,0:T(8,128)(2,1)} %bitcast.19), calls=%async_computation.2 | async-start | bytes 3145728 | tf_op jit(solution)/shard_map/all_to_all | solution.py:246
  169.3 367.9 %all-gather.18.cloned.1.call-start = ((), (), s32[]{:S(2)}) async-start(), calls=%async_computation.15 | async-start | bytes 3244032 | tf_op jit(solution)/shard_map/all_gather | solution.py:83
  189.5 23.6 %all-to-all-start = ((bf16[8,128,768]{2,1,0:T(8,128)(2,1)}), bf16[8,128,768]{2,1,0:T(8,128)(2,1)S(1)}, u32[]{:S(2)}, u32[]{:S(2)}) async-start(bf16[8,128,768]{2,1,0:T(8,128)(2,1)} %bitcast.220), calls=%async_computation | async-start | bytes 3145728 | tf_op jit(solution)/shard_map/all_to_all | solution.py:186
  193.1 628.3 %reduce-scatter.18.cloned.1.call-start = ((), (), s32[]{:S(2)}) async-start(), calls=%async_computation.21 | async-start | bytes 7077888 | tf_op jit(solution)/shard_map/reduce_scatter | solution.py:313
  307.3 99.3 %copy-start.21 = (bf16[2,4,128,768]{3,2,1,0:T(8,128)(2,1)S(1)}, bf16[2,4,128,768]{3,2,1,0:T(8,128)(2,1)}, u32[]{:S(2)}) copy-start(bf16[2,4,128,768]{3,2,1,0:T(8,128)(2,1)} %copy.139) | copy-start | bytes 4718596
  428.5 439.9 %reduce-scatter.16.cloned.1.call-start = ((), (), s32[]{:S(2)}) async-start(), calls=%async_computation.20 | async-start | bytes 14155776 | tf_op jit(solution)/shard_map/reduce_scatter | solution.py:310
  443.0 94.3 %copy-start.3 = (bf16[512,768]{1,0:T(8,128)(2,1)S(1)}, bf16[512,768]{1,0:T(8,128)(2,1)}, u32[]{:S(2)}) copy-start(bf16[512,768]{1,0:T(8,128)(2,1)} %param.20) | copy-start | bytes 2359300
  443.0 545.3 %reduce-scatter.14.cloned.1.call-start = ((), (), s32[]{:S(2)}) async-start(), calls=%async_computation.19 | async-start | bytes 6488064 | tf_op jit(solution)/shard_map/reduce_scatter | solution.py:307
  562.7 23.8 %all-to-all-start.1 = ((bf16[2,512,768]{2,0,1:T(2,128)(2,1)}), bf16[2,512,768]{2,0,1:T(2,128)(2,1)S(1)}, u32[]{:S(2)}, u32[]{:S(2)}) async-start(bf16[2,512,768]{2,0,1:T(2,128)(2,1)} %copy.134), calls=%async_computation.1 | async-start | bytes 3145728 | tf_op jit(solution)/shard_map/all_to_all | solution.py:196
  586.5 34.5 %all-to-all-start.3 = ((bf16[2,512,768]{2,0,1:T(2,128)(2,1)}), bf16[2,512,768]{2,0,1:T(2,128)(2,1)}, u32[]{:S(2)}, u32[]{:S(2)}) async-start(bf16[2,512,768]{2,0,1:T(2,128)(2,1)} %copy.140), calls=%async_computation.3 | async-start | bytes 3145728 | tf_op jit(solution)/shard_map/all_to_all | solution.py:262
  590.8 502.2 %reduce-scatter.10.cloned.1.call-start = ((), (), s32[]{:S(2)}) async-start(), calls=%async_computation.17 | async-start | bytes 2433024 | tf_op jit(solution)/shard_map/reduce_scatter | solution.py:304
  605.4 5.0 copy-start.4
  633.3 7.0 copy-start.1
  643.0 1.6 copy-start.11
  646.8 607.2 %reduce-scatter.12.cloned.1.call-start = ((), (), s32[]{:S(2)}) async-start(), calls=%async_computation.18 | async-start | bytes 12976128 | tf_op jit(solution)/shard_map/reduce_scatter | solution.py:306
  655.6 723.9 %reduce-scatter.8.cloned.1.call-start = ((), (), s32[]{:S(2)}) async-start(), calls=%async_computation.16 | async-start | bytes 7299072 | tf_op jit(solution)/shard_map/reduce_scatter | solution.py:303
  659.1 2.4 copy-start.9
  661.5 91.6 %copy-start.26 = (f32[512,64]{0,1:T(8,128)S(1)}, f32[512,64]{0,1:T(8,128)}, u32[]{:S(2)}) copy-start(f32[512,64]{0,1:T(8,128)} %copy-done.25) | copy-start | bytes 393220
  753.1 2.7 copy-start.24
  755.6 1.4 copy-start.5
  755.6 1.9 copy-start.6
  757.5 2.1 copy-start.15
  757.5 2.1 copy-start.31
  757.5 2.1 copy-start.33
  764.9 48.1 %copy-start.16 = (bf16[512,768]{1,0:T(8,128)(2,1)S(1)}, bf16[512,768]{1,0:T(8,128)(2,1)}, u32[]{:S(2)}) copy-start(bf16[512,768]{1,0:T(8,128)(2,1)} %param.17) | copy-start | bytes 2359300
  812.9 3.8 copy-start.19
  812.9 3.8 copy-start.22
  (6 other events, 7.0 us)
Sparse Core Ops, SparseCore 0:
  10.9 63.0 all-gather.7
  76.9 52.8 all-gather.9
  132.0 175.2 all-gather.11
  309.4 97.2 all-gather.13
  409.3 67.6 all-gather.15
  479.8 57.4 all-gather.17
  540.8 116.7 reduce-scatter.17
  661.2 207.1 reduce-scatter.15
  874.6 113.6 reduce-scatter.13
  994.8 98.1 reduce-scatter.9
  1099.7 154.3 reduce-scatter.11
  1261.2 118.3 reduce-scatter.7
where the time goes:
time: 1390 us
  waiting for transfers between devices  848 us (61%)
  matrix products  250 us (18%)
  blocking collectives  123 us (9%)
  local copies, waits for them, and re-layouts  80.3 us (6%)
  other arithmetic  53.4 us (4%)
  starting transfers between devices  16.5 us (1%)
  between operations  15.1 us (1%)
    reduce_scatter x1, waiting for transfers between devices, body(): lax.psum_scatter(shared_gate_up_grad, ('dp', 'expert'), scatter_dimension...  161 us
    reduce_scatter x1, waiting for transfers between devices, body(): lax.psum_scatter(qkv_grad, ('dp', 'expert'), scatter_dimension=0, tiled=T...  125 us
    reduce_scatter x1, waiting for transfers between devices, body(): lax.psum_scatter(shared_down_grad, ('dp', 'expert'), scatter_dimension=0,...  116 us
    reduce_scatter x1, waiting for transfers between devices, body(): lax.psum_scatter(out_weight_grad, ('dp', 'expert'), scatter_dimension=0,...  105 us
    all_gather x1, waiting for transfers between devices, body(): lax.all_gather(expert_gate_up, 'dp', axis=1, tiled=True)  92.9 us
    all_gather x1, waiting for transfers between devices, body(): lax.all_gather(expert_down, 'dp', axis=1, tiled=True)  83.9 us
    unnamed x2, blocking collectives  81.8 us
    all_gather x1, waiting for transfers between devices, body(): lax.all_gather(shared_down, ('dp', 'expert'), axis=0, tiled=True)  51.7 us
  transfers between devices with their start and end apart: 16, of which 12 were waited for; matrix products, arithmetic and copies ran while one was open for 27% of the time, Pallas kernels for 0%

commit v1 on v0

v1 whole, which is shorter than its diff:
```python
import functools

import jax
import jax.numpy as jnp
from jax import lax
from jax.experimental import pallas as pl
from jax.experimental.pallas import tpu as pltpu
from jax.sharding import PartitionSpec as P

D = 768
HEADS = 12
HEAD_DIM = 64
FF = 2048
CHUNK = 256
AX = ("dp", "expert")
PAIR_LOW = False

epsilon = 1e-06
bf16 = jnp.bfloat16
f32 = jnp.float32


def dot(left, right, left_dim, right_dim, precision=None):
    return lax.dot_general(
        left,
        right,
        (((left_dim,), (right_dim,)), ((), ())),
        preferred_element_type=f32,
        precision=precision,
    )


def rope_tables(length, head_width):
    half_width = head_width // 2
    frequency = 10000.0 ** (-jnp.arange(half_width, dtype=jnp.float32) / half_width)
    angles = jnp.arange(length, dtype=jnp.float32)[:, None] * frequency[None, :]
    angles = jnp.concatenate([angles, angles], axis=-1)[:, None, :]
    return (jnp.cos(angles), jnp.sin(angles))


def rotate(values, cosine_table, sine_table):
    half_width = values.shape[-1] // 2
    turned = jnp.concatenate([-values[..., half_width:], values[..., :half_width]], axis=-1)
    return values * cosine_table + turned * sine_table


def rotate_back(grads, cosine_table, sine_table):
    half_width = grads.shape[-1] // 2
    sined = grads * sine_table
    return grads * cosine_table + jnp.concatenate(
        [sined[..., half_width:], -sined[..., :half_width]], axis=-1
    )


def norm_back(grad_normed, normed, scale):
    return scale * (grad_normed - normed * jnp.mean(grad_normed * normed, axis=-1, keepdims=True))


def unpermute(values, order):
    high = values.astype(bf16)
    rest = (values - high.astype(f32)).astype(bf16)
    return dot(high, order, 1, 1) + dot(rest, order, 1, 1)


def two_layer_kernel(
    where_ref,
    a_ref,
    b_ref,
    x_ref,
    u_ref,
    w_ref,
    order_ref,
    gate_ref,
    up_ref,
    down_ref,
    *refs,
    routed,
    subs,
):
    if routed:
        out_ref, dx_ref, gg_ref, dgu_ref, dd_ref, xp, go, out_sum, dx_sum = refs
    else:
        out_ref, dx_ref, dgu_ref, dd_ref, xp, go, out_sum, dx_sum = refs
    step = pl.program_id(0)

    @pl.when(step == 0)
    def _():
        xp[...] = dot(x_ref[...], order_ref[...], 1, 0).astype(bf16)
        if routed:
            go[...] = (u_ref[...].astype(f32) * w_ref[...]).astype(bf16)
        else:
            go[...] = u_ref[...]

    x = xp[...]
    grad_out = go[...]
    cores, lanes = 2, subs // 2
    sub_x, sub_c = where_ref[0], where_ref[1]
    places = []
    for n in range(subs):
        places.append((lax.bitwise_xor(n % cores, sub_c), lax.bitwise_xor(n // cores, sub_x)))
    down = jnp.concatenate([down_ref[i, 0, j, 0] for i, j in places], axis=0)
    gate = dot(x, gate_ref[...], 1, 0)
    up = dot(x, up_ref[...], 1, 0)
    sigmoid = jax.nn.sigmoid(gate)
    act = gate * sigmoid
    slope = sigmoid * (1.0 + gate * (1.0 - sigmoid))
    hidden = (act * up).astype(bf16)
    out_part = dot(hidden, down, 1, 0)
    grad_hidden = dot(grad_out, down, 1, 1)
    grad_gate = (grad_hidden * up * slope).astype(bf16)
    grad_up = (grad_hidden * act).astype(bf16)
    dx_part = dot(grad_gate, gate_ref[...], 1, 1) + dot(grad_up, up_ref[...], 1, 1)
    grad_down = dot(hidden, grad_out, 0, 0).astype(bf16)
    rows = grad_down.shape[0] // subs
    for n, (i, j) in enumerate(places):
        dd_ref[i, 0, j, 0] = grad_down[n * rows : (n + 1) * rows]
    blocks, _, per, _ = dgu_ref.shape
    for half, grads in ((0, grad_gate), (1, grad_up)):
        weight_grad = dot(x, grads, 0, 0).astype(bf16)
        for n in range(blocks):
            dgu_ref[n, half] = weight_grad[n * per : (n + 1) * per]

    @pl.when(step == 0)
    def _():
        out_sum[...] = out_part
        dx_sum[...] = dx_part

    @pl.when(step > 0)
    def _():
        out_sum[...] += out_part
        dx_sum[...] += dx_part

    @pl.when(step == pl.num_programs(0) - 1)
    def _():
        if routed:
            out_low = out_sum[...].astype(bf16)
            out_ref[...] = out_low
            gg_ref[...] = jnp.sum(u_ref[...].astype(f32) * out_low.astype(f32), axis=1, keepdims=True)
            dx_ref[...] = dot(dx_sum[...].astype(bf16), order_ref[...], 1, 1).astype(bf16)
        else:
            out_ref[...] = out_sum[...]
            dx_ref[...] = unpermute(dx_sum[...], order_ref[...])


def two_layers(where, a_index, b_index, x, u, w, order, gate_up, down, blocks, routed):
    rows = x.shape[0]
    cores, a_size, lanes, b_size, per_down, _ = down.shape
    chunks = a_size * b_size
    width = FF // chunks
    per = D // blocks
    whole = lambda *shape: pl.BlockSpec(shape, lambda s, *_: (0,) * len(shape))
    down_spec = pl.BlockSpec(
        (cores, 1, lanes, 1, per_down, D), lambda s, q, a, b: (0, a[s], 0, b[s], 0, 0)
    )
    kind = bf16 if routed else f32
    outs = [
        jax.ShapeDtypeStruct((rows, D), kind),
        jax.ShapeDtypeStruct((rows, D), kind),
        jax.ShapeDtypeStruct((blocks, 2, per, FF), bf16),
        jax.ShapeDtypeStruct(down.shape, bf16),
    ]
    out_specs = [
        whole(rows, D),
        whole(rows, D),
        pl.BlockSpec((blocks, 2, per, width), lambda s, *_: (0, 0, 0, s)),
        down_spec,
    ]
    if routed:
        outs.insert(2, jax.ShapeDtypeStruct((rows, 1), f32))
        out_specs.insert(2, whole(rows, 1))
    return pl.pallas_call(
        functools.partial(two_layer_kernel, routed=routed, subs=cores * lanes),
        grid_spec=pltpu.PrefetchScalarGridSpec(
            num_scalar_prefetch=3,
            grid=(chunks,),
            in_specs=[
                whole(rows, D),
                whole(rows, D),
                whole(rows, 1),
                whole(D, D),
                pl.BlockSpec((D, width), lambda s, *_: (0, s)),
                pl.BlockSpec((D, width), lambda s, *_: (0, s + chunks)),
                down_spec,
            ],
            out_specs=out_specs,
            scratch_shapes=[
                pltpu.VMEM((rows, D), bf16),
                pltpu.VMEM((rows, D), bf16),
                pltpu.VMEM((rows, D), f32),
                pltpu.VMEM((rows, D), f32),
            ],
        ),
        out_shape=outs,
        compiler_params=pltpu.CompilerParams(vmem_limit_bytes=56 << 20),
        cost_estimate=pl.CostEstimate(
            flops=2 * 9 * rows * D * FF,
            bytes_accessed=12 * D * FF + 12 * rows * D,
            transcendentals=rows * FF,
        ),
        name="two_layers",
    )(where, a_index, b_index, x, u, w, order, gate_up, gate_up, down)


def body(
    dp_size,
    expert_size,
    tokens,
    segment_ids,
    expert_ids,
    upstream,
    norm_first,
    qkv_weight,
    out_weight,
    norm_second,
    router_weight,
    shared_gate_up,
    shared_down,
    expert_gate_up,
    expert_down,
):
    devices = dp_size * expert_size
    lanes = expert_size // 2
    length = tokens.shape[0]
    experts = expert_gate_up.shape[0] * expert_size
    held = expert_gate_up.shape[0]
    group = experts // lanes
    pairs = dp_size // group
    capacity = length * 2 // experts
    score_scale = HEAD_DIM ** (-0.5)
    tall = dp_size // 2

    me = lax.axis_index(AX).astype(jnp.int32)
    my_dp, my_expert = me // expert_size, me % expert_size
    my_x, my_c = my_expert // 2, my_expert % 2
    if PAIR_LOW:
        pair_of, group_of = (lambda d: d % pairs), (lambda d: d // pairs)
        dp_of = lambda p, g: g * pairs + p
    else:
        pair_of, group_of = (lambda d: d // group), (lambda d: d % group)
        dp_of = lambda p, g: p * group + g
    my_p, my_g = pair_of(my_dp), group_of(my_dp)

    def hop(values, offset):
        return lax.ppermute(values, AX, [(s, s ^ offset) for s in range(devices)])

    def spread(values, offsets):
        return jnp.stack([values] + [hop(values, o) for o in offsets[1:]])

    def collect(blocks, offsets):
        total = blocks[0].astype(f32)
        for i, o in enumerate(offsets[1:]):
            total = total + hop(blocks[i + 1], o).astype(f32)
        return total

    tall_offsets = [2 * i * expert_size for i in range(tall)]
    flat_offsets = [y * expert_size + 2 * x for y in range(2) for x in range(lanes)]
    pair_offsets = [dp_of(p, 0) * expert_size for p in range(pairs)]
    group_offsets = [dp_of(0, g) * expert_size for g in range(group)]
    owner_offsets = [dp_of(0, g) * expert_size + 2 * x for g in range(group) for x in range(lanes)]

    def gather_dense(shard):
        return spread(spread(spread(shard, tall_offsets), flat_offsets), [0, 1])

    def scatter_dense(grads):
        grads = collect(grads, [0, 1]).astype(bf16)
        grads = collect(grads, flat_offsets).astype(bf16)
        return collect(grads, tall_offsets)

    def dense_home(position):
        i, j, c = position % tall, position // tall % (2 * lanes), position // tall // (2 * lanes)
        offset = (2 * i + j // lanes) * expert_size + 2 * (j % lanes) + c
        return lax.bitwise_xor(me, offset)

    def gather_expert(shard):
        halves = shard.reshape(held, 2, shard.shape[1] // 2, shard.shape[2])
        mine = lax.dynamic_index_in_dim(halves, my_c, 1, keepdims=False)
        other = hop(lax.dynamic_index_in_dim(halves, 1 - my_c, 1, keepdims=False), 1)
        all_held = jnp.concatenate(
            [jnp.where(my_c == 0, mine, other), jnp.where(my_c == 0, other, mine)], axis=0
        )
        parts = [
            lax.dynamic_index_in_dim(all_held, lax.bitwise_xor(my_g, g), 0, keepdims=False)
            for g in range(group)
        ]
        parts = jnp.stack([parts[0]] + [hop(parts[g], group_offsets[g]) for g in range(1, group)])
        return spread(spread(parts, pair_offsets), [0, 1])

    def scatter_expert(grads):
        grads = collect(grads, [0, 1]).astype(bf16)
        grads = collect(grads, pair_offsets).astype(bf16)
        parts = jnp.stack([grads[0]] + [hop(grads[g], group_offsets[g]) for g in range(1, group)])
        keep = [
            lax.dynamic_index_in_dim(parts, lax.bitwise_xor(my_g, my_c * held + j), 0)
            for j in range(held)
        ]
        give = [
            lax.dynamic_index_in_dim(parts, lax.bitwise_xor(my_g, (1 - my_c) * held + j), 0)
            for j in range(held)
        ]
        keep = jnp.concatenate(keep, axis=0)
        take = hop(jnp.concatenate(give, axis=0), 1)
        return jnp.stack([jnp.where(my_c == 0, keep, take), jnp.where(my_c == 0, take, keep)], axis=1)

    def expert_home(position):
        g, p, c = position % group, position // group % pairs, position // group // pairs
        dp = dp_of(lax.bitwise_xor(my_p, p), lax.bitwise_xor(my_g, g))
        return dp * 2 + lax.bitwise_xor(my_c, c)

    def order_of(home, blocks, width=D):
        per = width // blocks
        column = jnp.arange(width, dtype=jnp.int32)
        source = home(column // per) * per + column % per
        return (jnp.arange(width, dtype=jnp.int32)[:, None] == source[None, :]).astype(bf16)

    def exchange(blocks):
        return [blocks[0]] + [
            hop(b, o) for b, o in zip(blocks[1:], owner_offsets[1:], strict=True)
        ]

    dense_order = order_of(dense_home, devices)
    expert_order = order_of(expert_home, 2 * dp_size)

    small = jnp.concatenate(
        [norm_first[:, None], norm_second[:, None], router_weight], axis=1
    )
    small = jnp.pad(small, ((0, 0), (0, 128 - small.shape[1])))
    qkv_full = gather_dense(jnp.concatenate([qkv_weight, small], axis=1)).reshape(D, 3 * D + 128)
    out_full = gather_dense(out_weight).reshape(D, D)
    shared_gu_full = gather_dense(shared_gate_up).reshape(D, 2 * FF)
    shared_down_full = gather_dense(shared_down)
    expert_gu_full = gather_expert(expert_gate_up).reshape(D, 2 * FF)
    expert_down_full = gather_expert(expert_down)

    columns = jnp.arange(experts, dtype=jnp.int32)
    pickers = [(expert_ids[:, j : j + 1] == columns[None, :]).astype(f32) for j in range(2)]
    position = jnp.arange(length)
    earlier = (position[:, None] > position[None, :]).astype(bf16)
    counts = dot(earlier, (pickers[0] + pickers[1]).astype(bf16), 1, 0)
    kept, places = [], []
    for j in range(2):
        rank = jnp.sum(counts * pickers[j], axis=1).astype(jnp.int32)
        ids = expert_ids[:, j]
        kept_mask = rank < capacity
        block = lax.bitwise_xor(ids % group, my_g) * lanes + lax.bitwise_xor(ids // group, my_x)
        slot = jnp.where(kept_mask, block * capacity + rank, -1)
        kept.append(kept_mask.astype(f32))
        places.append(
            (slot[:, None] == jnp.arange(experts * capacity, dtype=jnp.int32)[None, :]).astype(bf16)
        )
    both_places = places[0] + places[1]

    def send_rows(values):
        rows = dot(both_places, values, 0, 0).astype(bf16).reshape(experts, capacity, D)
        return jnp.concatenate(exchange([rows[k] for k in range(experts)]), axis=0)

    upstream_rows = send_rows(upstream)

    small_full = dot(qkv_full[:, 3 * D :], dense_order, 0, 1)
    gain_one, gain_two = small_full[0:1], small_full[1:2]
    router_full = small_full[2 : 2 + experts].astype(bf16)
    stream = tokens.astype(f32)
    scale_one = lax.rsqrt(jnp.mean(stream * stream, axis=-1, keepdims=True) + epsilon)
    normed_one = stream * scale_one
    normed_low = (normed_one * gain_one).astype(bf16)
    normed_low = dot(normed_low, dense_order, 1, 0).astype(bf16)
    projected = dot(normed_low, qkv_full[:, : 3 * D], 1, 0)
    cosine_table, sine_table = rope_tables(length, HEAD_DIM)
    query_rot = rotate(
        projected[:, :D].reshape(length, HEADS, HEAD_DIM), cosine_table, sine_table
    ).astype(bf16)
    key_rot = rotate(
        projected[:, D : 2 * D].reshape(length, HEADS, HEAD_DIM), cosine_table, sine_table
    ).astype(bf16)
    value_low = projected[:, 2 * D :].astype(bf16).reshape(length, HEADS, HEAD_DIM)
    query_heads = jnp.swapaxes(query_rot, 0, 1)
    key_heads = jnp.swapaxes(key_rot, 0, 1)
    value_heads = jnp.swapaxes(value_low, 0, 1)
    segments = segment_ids[0]
    allowed = (position[:, None] >= position[None, :]) & (segments[:, None] == segments[None, :])

    def head_scores(query_head, key_head):
        scores = dot(query_head, key_head, 1, 1) * score_scale
        return jnp.where(allowed, scores, -1000000000.0)

    def head_forward(parts):
        query_head, key_head, value_head = parts
        scores = head_scores(query_head, key_head)
        top_score = jnp.max(scores, axis=-1, keepdims=True)
        exp_scores = jnp.exp(scores - top_score)
        row_total = jnp.sum(exp_scores, axis=-1, keepdims=True)
        attn_probs = exp_scores / row_total
        head_out = dot(attn_probs.astype(bf16), value_head, 1, 0)
        return (head_out, (top_score + jnp.log(row_total))[:, 0])

    def head_backward(parts):
        query_head, key_head, value_head, grad_head, log_total = parts
        scores = head_scores(query_head, key_head)
        attn_probs = jnp.exp(scores - log_total[:, None])
        grad_value = dot(attn_probs.astype(bf16), grad_head, 0, 0)
        grad_probs = dot(grad_head, value_head, 1, 1)
        grad_scores = attn_probs * (
            grad_probs - jnp.sum(grad_probs * attn_probs, axis=-1, keepdims=True)
        )
        grad_low = grad_scores.astype(bf16)
        grad_query = dot(grad_low, key_head, 1, 0) * score_scale
        grad_key = dot(grad_low, query_head, 0, 0) * score_scale
        return (grad_query, grad_key, grad_value)

    head_outs, log_totals = lax.map(head_forward, (query_heads, key_heads, value_heads))
    attended = jnp.swapaxes(head_outs, 0, 1).reshape(length, D).astype(bf16)
    attended = dot(attended, dense_order, 1, 0).astype(bf16)
    stream_mid = stream + dot(attended, out_full, 1, 0)
    scale_two = lax.rsqrt(jnp.mean(stream_mid * stream_mid, axis=-1, keepdims=True) + epsilon)
    normed_two = stream_mid * scale_two
    expert_in = (normed_two * gain_two).astype(bf16)
    logits = dot(expert_in, router_full, 1, 1)
    chosen = jnp.stack([jnp.sum(p * logits, axis=-1) for p in pickers], axis=1)
    chosen_top = jnp.max(chosen, axis=1, keepdims=True)
    chosen_exp = jnp.exp(chosen - chosen_top)
    gate_values = chosen_exp / jnp.sum(chosen_exp, axis=1, keepdims=True)
    kept_float = jnp.stack(kept, axis=1)
    mix_weight = kept_float * gate_values

    arrived = send_rows(expert_in)
    slot_weight = sum(
        jnp.sum(places[j].astype(f32) * mix_weight[:, j : j + 1], axis=0) for j in range(2)
    ).reshape(experts, 1, capacity)
    slot_weight = jnp.concatenate(exchange([slot_weight[k] for k in range(experts)]), axis=0)
    chunk_ids = jnp.arange(dp_size, dtype=jnp.int32)
    if FF // dp_size == CHUNK:
        expert_down_in = expert_down_full.reshape(2, pairs, 1, group, CHUNK // 2, D)
        expert_a = lax.bitwise_xor(pair_of(chunk_ids), my_p)
        expert_b = lax.bitwise_xor(group_of(chunk_ids), my_g)
        expert_where = jnp.stack([jnp.zeros_like(my_c), my_c])
        shared_down_in = shared_down_full.reshape(2, 2, lanes, tall, CHUNK // expert_size, D)
        shared_a = lax.bitwise_xor(chunk_ids % 2, my_dp % 2)
        shared_b = lax.bitwise_xor(chunk_ids // 2, my_dp // 2)
        shared_where = jnp.stack([my_x, my_c])
    else:
        natural = (FF // CHUNK, 2, CHUNK // 2, D)
        expert_rows = order_of(expert_home, 2 * dp_size, FF)
        dense_rows = order_of(dense_home, devices, FF)
        expert_down_in = dot(expert_rows, expert_down_full.reshape(FF, D), 1, 0).astype(bf16)
        expert_down_in = expert_down_in.reshape(natural).swapaxes(0, 1)[:, None, None]
        shared_down_in = dot(dense_rows, shared_down_full.reshape(FF, D), 1, 0).astype(bf16)
        shared_down_in = shared_down_in.reshape(natural).swapaxes(0, 1)[:, None, None]
        chunk_ids = jnp.arange(FF // CHUNK, dtype=jnp.int32)
        expert_a = shared_a = jnp.zeros_like(chunk_ids)
        expert_b = shared_b = chunk_ids
        expert_where = shared_where = jnp.zeros((2,), jnp.int32)
    expert_blocks = 2 * dp_size if (D // (2 * dp_size)) % 16 == 0 else 2
    shared_blocks = 4 * lanes if (D // (4 * lanes)) % 16 == 0 else 2
    expert_out, grad_rows, grad_gates, expert_gu_grad, expert_down_grad = two_layers(
        expert_where,
        expert_a,
        expert_b,
        arrived,
        upstream_rows,
        slot_weight.reshape(experts * capacity, 1),
        expert_order,
        expert_gu_full,
        expert_down_in,
        expert_blocks,
        True,
    )
    shared_out, shared_dx, shared_gu_grad, shared_down_grad = two_layers(
        shared_where,
        shared_a,
        shared_b,
        expert_in,
        upstream,
        jnp.ones((length, 1), f32),
        dense_order,
        shared_gu_full,
        shared_down_in,
        shared_blocks,
        False,
    )

    def return_rows(values):
        values = values.reshape((experts, capacity) + values.shape[1:])
        return jnp.concatenate(exchange([values[k] for k in range(experts)]), axis=0)

    grad_gates = grad_gates.reshape(experts, 1, capacity)
    gate_back = jnp.concatenate(exchange([grad_gates[k] for k in range(experts)]), axis=0)
    buffer_rows = return_rows(grad_rows)
    returned = return_rows(expert_out)
    mixed = stream_mid + shared_out
    for j in range(2):
        mixed = mixed + mix_weight[:, j : j + 1] * dot(places[j], returned, 1, 0)
    mixed = mixed.astype(bf16)

    cotangent = upstream.astype(f32)
    gate_row = gate_back.reshape(1, experts * capacity)
    grad_gate = jnp.stack(
        [jnp.sum(places[j].astype(f32) * gate_row, axis=1) for j in range(2)], axis=1
    )
    grad_chosen = gate_values * (
        grad_gate - jnp.sum(gate_values * grad_gate, axis=1, keepdims=True)
    )
    grad_logits = sum(pickers[j] * grad_chosen[:, j : j + 1] for j in range(2)).astype(bf16)
    expert_in_ordered = dot(expert_in, dense_order, 1, 0).astype(bf16)
    router_grad = dot(expert_in_ordered, grad_logits, 0, 0)
    grad_expert_in = (
        shared_dx + dot(grad_logits, router_full, 1, 0) + dot(both_places, buffer_rows, 1, 0)
    )
    norm_second_grad = jnp.sum(grad_expert_in * normed_two, axis=0, keepdims=True)
    grad_mid = cotangent + norm_back(grad_expert_in * gain_two, normed_two, scale_two)
    grad_mid_low = grad_mid.astype(bf16)
    out_weight_grad = dot(attended, grad_mid_low, 0, 0)
    grad_attended = dot(grad_mid_low, out_full, 1, 1).astype(bf16)
    grad_attended = dot(grad_attended, dense_order, 1, 1).astype(bf16)
    grad_heads = jnp.swapaxes(grad_attended.reshape(length, HEADS, HEAD_DIM), 0, 1)
    grad_query, grad_key, grad_value = lax.map(
        head_backward, (query_heads, key_heads, value_heads, grad_heads, log_totals)
    )
    grad_query = rotate_back(jnp.swapaxes(grad_query, 0, 1), cosine_table, sine_table).reshape(
        length, D
    )
    grad_key = rotate_back(jnp.swapaxes(grad_key, 0, 1), cosine_table, sine_table).reshape(
        length, D
    )
    grad_value = jnp.swapaxes(grad_value, 0, 1).reshape(length, D)
    grad_projected = jnp.concatenate([grad_query, grad_key, grad_value], axis=-1).astype(bf16)
    qkv_grad = dot(normed_low, grad_projected, 0, 0)
    grad_normed = unpermute(dot(grad_projected, qkv_full[:, : 3 * D], 1, 1), dense_order)
    norm_first_grad = jnp.sum(grad_normed * normed_one, axis=0, keepdims=True)
    input_grad = grad_mid + norm_back(grad_normed * gain_one, normed_one, scale_one)

    def to_rows(row):
        high = row.astype(bf16)
        rest = (row - high.astype(f32)).astype(bf16)
        return dot(dense_order, high, 0, 1) + dot(dense_order, rest, 0, 1)

    def relative(grads):
        return grads.astype(bf16).reshape(2, 2 * lanes, tall, -1, grads.shape[-1])

    out_pack = jnp.concatenate(
        [
            out_weight_grad,
            jnp.pad(
                jnp.concatenate([to_rows(norm_second_grad), router_grad], axis=1),
                ((0, 0), (0, 127 - experts)),
            ),
        ],
        axis=1,
    )
    qkv_pack = jnp.concatenate(
        [qkv_grad, jnp.pad(to_rows(norm_first_grad), ((0, 0), (0, 127)))], axis=1
    )
    if expert_blocks == 2 * dp_size:
        expert_gu_grad = expert_gu_grad.reshape(2, pairs, group, 2, -1, FF)
    else:
        expert_gu_grad = expert_gu_grad.reshape(2, 2, pairs, group, -1, FF)
        expert_gu_grad = jnp.moveaxis(expert_gu_grad, 1, 3)
    shared_gu_grad = shared_gu_grad.reshape(
        (2, 2 * lanes, 2, tall, -1, FF)
        if shared_blocks == 4 * lanes
        else (2, 2, 2 * lanes, tall, -1, FF)
    )
    shared_gu_grad = jnp.moveaxis(shared_gu_grad, 2 if shared_blocks == 4 * lanes else 1, 3)
    if FF // dp_size == CHUNK:
        expert_down_grad = expert_down_grad.reshape(2, pairs, group, CHUNK // 2, D)
        shared_down_grad = shared_down_grad.reshape(2, 2 * lanes, tall, -1, D)
    else:
        expert_down_grad = expert_down_grad.reshape(2, -1, CHUNK // 2, D).swapaxes(0, 1)
        shared_down_grad = shared_down_grad.reshape(2, -1, CHUNK // 2, D).swapaxes(0, 1)
        expert_down_grad = dot(expert_rows, expert_down_grad.reshape(FF, D), 0, 0).astype(bf16)
        expert_down_grad = expert_down_grad.reshape(2, pairs, group, -1, D)
        shared_down_grad = dot(dense_rows, shared_down_grad.reshape(FF, D), 0, 0).astype(bf16)
        shared_down_grad = shared_down_grad.reshape(2, 2 * lanes, tall, -1, D)
    expert_gu_sum = scatter_expert(expert_gu_grad)
    expert_down_sum = scatter_expert(expert_down_grad)
    shared_gu_sum = scatter_dense(shared_gu_grad)
    shared_down_sum = scatter_dense(shared_down_grad)
    out_sum = scatter_dense(relative(out_pack))
    qkv_sum = scatter_dense(relative(qkv_pack))
    expert_gu_sum = jnp.moveaxis(expert_gu_sum, 2, 3).reshape(held, -1, 2 * FF).astype(f32)
    return (
        mixed,
        input_grad,
        qkv_sum[:, 3 * D],
        qkv_sum[:, : 3 * D],
        out_sum[:, :D],
        out_sum[:, D],
        out_sum[:, D + 1 : D + 1 + experts],
        jnp.moveaxis(shared_gu_sum, 0, 1).reshape(-1, 2 * FF),
        shared_down_sum,
        expert_gu_sum,
        expert_down_sum.reshape(held, -1, D).astype(f32),
    )


def solution(mesh):
    rows = P(AX, None)
    split = P("expert", "dp", None)
    in_specs = (rows,) * 4 + (P(AX), rows, rows, P(AX)) + (rows,) * 3 + (split,) * 2
    out_specs = (rows, rows, P(AX), rows, rows, P(AX)) + (rows,) * 3 + (split,) * 2
    inner = functools.partial(body, mesh.shape["dp"], mesh.shape["expert"])
    return jax.shard_map(inner, mesh=mesh, in_specs=in_specs, out_specs=out_specs, check_vma=False)
```

time: 1390 us -> 894 us (0.64)
  waiting for transfers between devices: 848 us -> 282 us
  starting transfers between devices: 16.5 us -> 155 us
  blocking collectives: 123 us -> 0 us
  matrix products: 250 us -> 165 us
  Pallas kernels: 0 us -> 81.3 us
  other arithmetic: 53.4 us -> 88.5 us
  local copies, waits for them, and re-layouts: 80.3 us -> 110 us
    reduce_scatter x6 -> x0, waiting for transfers between devices: 552 us -> none  [the longest x1 161 us: body(): lax.psum_scatter(shared_gate_up_grad, ('dp', 'expert'), scatter_dimension...]
    ppermute x0 -> x122, waiting for transfers between devices: none -> 282 us  [hop(): return lax.ppermute(values, AX, [(s, s ^ offset) for s in range(devices)])]
    all_gather x6 -> x0, waiting for transfers between devices: 263 us -> none  [the longest x1 92.9 us: body(): lax.all_gather(expert_gate_up, 'dp', axis=1, tiled=True)]
    ppermute x0 -> x122, starting transfers between devices: none -> 155 us  [hop(): return lax.ppermute(values, AX, [(s, s ^ offset) for s in range(devices)])]
    dot_general x105 -> x108, matrix products: 250 us -> 165 us  [dot(): lax.dot_general(left, right, (((left_dim,), (right_dim,)), ((), ())), pre...]
    unnamed x2 -> x0, blocking collectives: 81.8 us -> none
    pallas_call x0 -> x2, Pallas kernels: none -> 81.3 us  [two_layers(): pl.pallas_call(functools.partial(two_layer_kernel, routed=routed, subs=co...]
    all_gather x1 -> x0, blocking collectives: 40.9 us -> none  [body(): lax.all_gather(router_weight, ('dp', 'expert'), axis=0, tiled=True)]
  transfers between devices with their start and end apart: 16 -> 122, of which waited for: 12 -> 51; matrix products, arithmetic and copies ran while one was open for 27% -> 38% of each run, Pallas kernels for 0% -> 3%
where the time goes in v1:
time: 894 us; the launch traced here: 884 us
  waiting for transfers between devices  282 us (32%)
  matrix products  165 us (18%)
  starting transfers between devices  155 us (17%)
  local copies, waits for them, and re-layouts  110 us (12%)
  other arithmetic  88.5 us (10%)
  Pallas kernels  81.3 us (9%)
    ppermute x122, waiting for transfers between devices, hop(): return lax.ppermute(values, AX, [(s, s ^ offset) for s in range(devices)])  282 us
    dot_general x108, matrix products, dot(): lax.dot_general(left, right, (((left_dim,), (right_dim,)), ((), ())), pre...  165 us
    ppermute x122, starting transfers between devices, hop(): return lax.ppermute(values, AX, [(s, s ^ offset) for s in range(devices)])  155 us
    pallas_call x2, Pallas kernels, two_layers(): pl.pallas_call(functools.partial(two_layer_kernel, routed=routed, subs=co...  81.3 us
    another operation x18, other arithmetic, spread(): return jnp.stack([values] + [hop(values, o) for o in offsets[1:]])  35 us
    unnamed x206, local copies, waits for them, and re-layouts  34.5 us
  transfers between devices with their start and end apart: 122, of which 51 were waited for; matrix products, arithmetic and copies ran while one was open for 38% of the time, Pallas kernels for 3%

profile of v1, /device:TPU:0, one launch (start us, length us, event | category | flops | bytes accessed | tf_op | source)
XLA Modules:
  0.0 884.4 jit_solution(10586343423837952434)
XLA Ops:
  7.2 3.5 collective-permute-start.22
  24.6 3.8 collective-permute-start.1
  29.1 3.8 collective-permute-start.15
  33.0 3.9 collective-permute-done.1
  56.2 4.1 collective-permute-done.24
  61.5 6.2 collective-permute-done.25
  71.7 7.0 collective-permute-done.3
  80.5 8.9 %collective-permute-done.5 = bf16[4,24,2432]{2,1,0:T(8,128)(2,1)S(1)} collective-permute-done((bf16[4,24,2432]{2,1,0:T(8,128)(2,1)S(1)}, bf16[4,24,2432]{2,1,0:T(8,128)(2,1)S(1)}, u32[]{:S(2)}, u32[]{:S(2)}) %collective-permute-start.5) | collective-permute-done | bytes 466976 | tf_op jit(solution)/shard_map/ppermute | solution.py:244
  89.5 7.9 collective-permute-start.57
  113.4 26.6 %collective-permute-done.18 = bf16[4,24,4096]{2,1,0:T(8,128)(2,1)} collective-permute-done((bf16[4,24,4096]{2,1,0:T(8,128)(2,1)}, bf16[4,24,4096]{2,1,0:T(8,128)(2,1)}, u32[]{:S(2)}, u32[]{:S(2)}) %collective-permute-start.18) | collective-permute-done | bytes 786464 | tf_op jit(solution)/shard_map/ppermute | solution.py:244
  142.4 5.0 collective-permute-done.50
  149.6 4.4 fusion.264
  154.1 14.4 %collective-permute-done.51 = bf16[48,4096]{1,0:T(8,128)(2,1)S(1)} collective-permute-done((bf16[48,4096]{1,0:T(8,128)(2,1)S(1)}, bf16[48,4096]{1,0:T(8,128)(2,1)S(1)}, u32[]{:S(2)}, u32[]{:S(2)}) %collective-permute-start.51) | collective-permute-done | bytes 393248 | tf_op jit(solution)/shard_map/ppermute | solution.py:244
  168.5 6.0 collective-permute-done.52
  182.5 3.4 pad_maximum_fusion.4.down_ref
  205.6 46.0 %while.30 = (s32[]{:T(128)}, bf16[12,512,64]{1,2,0:T(8,128)(2,1)}, f32[12,512]{1,0:T(8,128)}, bf16[12,512,64]{2,1,0:T(8,128)(2,1)}, bf16[12,512,64]{2,1,0:T(8,12...) while((s32[]{:T(128)}, bf16[12,512,64]{1,2,0:T(8,128)(2,1)}, ...), condition=%wide.region_4.5_spmd.clone.clone, body=%wide.region_1.4_spmd.clone.sunk.clone | while | flops 69991936 | bytes 3696721 | solution.py:409
  288.5 3.6 collective-permute-done.39
  303.8 3.6 fusion.261
  307.5 5.2 pad_maximum_fusion
  313.4 30.0 %two_layers.2 = (f32[512,768]{1,0:T(8,128)}, f32[512,768]{1,0:T(8,128)}, bf16[8,2,96,2048]{3,2,1,0:T(8,128)(2,1)}, bf16[2,2,2,4,64,768]{5,4,3,2,1,0:T(8,128)(2,1)}) custom-call(s32[2]{0:T(128)} %pad_add_fusion.where_ref, s32[8]{0:T(128)} %get-tuple-element.489.a_ref, s32[8]{0:T(128)} %get-tuple-element.490.b_ref, bf16[512,768]{1,0:T(8,128)(2,1)} %copy-done.17, ...), custom_call_target="tpu_custom_call" | custom-call | flops 14495514624 | bytes 23592960 | tf_op jit(solution)/shard_map/two_layers/pallas_call | solution.py:171
  365.0 3.6 collective-permute-done.34
  376.5 5.1 pad_maximum_fusion.1
  381.5 51.3 %two_layers.3 = (bf16[1024,768]{1,0:T(8,128)(2,1)}, bf16[1024,768]{1,0:T(8,128)(2,1)}, f32[1024,1]{1,0:T(8,128)}, bf16[16,2,48,2048]{3,2,1,0:T(8,128)(2,1)}, bf16[2,2,1,4,128,768]{5,4,3,2,1,0:T(8,128)(2,1)}) custom-call(s32[2]{0:T(128)} %pad_add_fusion.1.where_ref, s32[8]{0:T(128)} %get-tuple-element.488.a_ref, s32[8]{0:T(128)} %get-tuple-element.487.b_ref, ...), custom_call_target="tpu_custom_call" | custom-call | flops 28991029248 | bytes 28311552 | tf_op jit(solution)/shard_map/two_layers/pallas_call | solution.py:171
  435.5 6.7 fusion.266
  464.4 6.3 collective-permute-done.75
  482.4 4.4 collective-permute-done.79
  496.4 3.5 multiply_reduce_fusion.1
  503.0 3.7 fusion.106
  509.0 107.4 %while.31 = (s32[]{:T(128)}, f32[12,512,64]{1,2,0:T(8,128)}, f32[12,512,64]{1,2,0:T(8,128)}, bf16[12,512,64]{1,2,0:T(8,128)(2,1)}, bf16[12,512,64]{2,1,0:T(8,128...) while((s32[]{:T(128)}, f32[12,512,64]{1,2,0:T(8,128)}, ...), condition=%wide.region_19.20_spmd.clone.clone, body=%wide.region_17.19_spmd.clone.sunk.clone | while | flops 170982912 | bytes 9063529 | solution.py:514
  621.9 3.3 convolution_convert_fusion
  638.5 3.5 collective-permute-done.63
  652.0 3.8 collective-permute-start.67
  667.7 3.6 fusion.90
  675.0 4.5 add_convert_fusion
  686.1 3.7 collective-permute-done.90
  698.5 6.1 collective-permute-done.108
  712.4 4.2 fusion.50
  725.8 11.6 %collective-permute-done.97 = bf16[4,2,24,2048]{3,2,0,1:T(8,128)(2,1)S(1)} collective-permute-done((bf16[4,2,24,2048]{3,2,0,1:T(8,128)(2,1)S(1)}, bf16[4,2,24,2048]{3,2,0,1:T(8,128)(2,1)S(1)}, u32[]{:S(2)}, u32[]{:S(2)}) %collective-permute-start.97) | collective-permute-done | bytes 786464 | tf_op jit(solution)/shard_map/ppermute | solution.py:244
  737.3 13.6 %collective-permute-done.98 = bf16[4,2,24,2048]{3,2,0,1:T(8,128)(2,1)S(1)} collective-permute-done((bf16[4,2,24,2048]{3,2,0,1:T(8,128)(2,1)S(1)}, bf16[4,2,24,2048]{3,2,0,1:T(8,128)(2,1)S(1)}, u32[]{:S(2)}, u32[]{:S(2)}) %collective-permute-start.98) | collective-permute-done | bytes 786464 | tf_op jit(solution)/shard_map/ppermute | solution.py:244
  750.9 4.5 collective-permute-done.99
  766.7 38.3 %collective-permute-done.101 = bf16[2,24,2048]{2,1,0:T(8,128)(2,1)S(1)} collective-permute-done((bf16[2,24,2048]{2,1,0:T(8,128)(2,1)S(1)}, bf16[2,24,2048]{2,1,0:T(8,128)(2,1)S(1)}, u32[]{:S(2)}, u32[]{:S(2)}) %collective-permute-start.101) | collective-permute-done | bytes 196640 | tf_op jit(solution)/shard_map/ppermute | solution.py:244
  808.1 3.3 collective-permute-start.119
  812.2 4.3 collective-permute-done.85
  816.8 25.2 %collective-permute-done.111 = bf16[4,2,48,2048]{3,2,1,0:T(8,128)(2,1)S(1)} collective-permute-done((bf16[4,2,48,2048]{3,2,1,0:T(8,128)(2,1)S(1)}, bf16[4,2,48,2048]{3,2,1,0:T(8,128)(2,1)S(1)}, u32[]{:S(2)}, u32[]{:S(2)}) %collective-permute-start.111) | collective-permute-done | bytes 1572896 | tf_op jit(solution)/shard_map/ppermute | solution.py:244
  846.6 4.9 collective-permute-done.120
  851.8 6.1 collective-permute-done.112
  861.3 12.1 %collective-permute-done.114 = bf16[2,48,2048]{2,1,0:T(8,128)(2,1)S(1)} collective-permute-done((bf16[2,48,2048]{2,1,0:T(8,128)(2,1)S(1)}, bf16[2,48,2048]{2,1,0:T(8,128)(2,1)S(1)}, u32[]{:S(2)}, u32[]{:S(2)}) %collective-permute-start.114) | collective-permute-done | bytes 393248 | tf_op jit(solution)/shard_map/ppermute | solution.py:244
  880.4 3.8 reshape.635
  (735 shorter events, 484.8 us)
Async XLA Ops:
  7.2 21.2 %collective-permute-start.22 = (bf16[64,768]{1,0:T(8,128)(2,1)}, bf16[64,768]{1,0:T(8,128)(2,1)S(1)}, u32[]{:S(2)}, u32[]{:S(2)}) collective-permute-start(bf16[64,768]{1,0:T(8,128)(2,1)} %param.27), channel_id=1, source_target_pairs={{0,16},{1,17},{2,18},{3,19},{4,20},{5,21},{6,22},{7,23},{8,24},{9,... | collective-permute-start | bytes 294920 | tf_op jit(solution)/shard_map/ppermute | solution.py:244
  20.4 21.0 %collective-permute-start.10 = (bf16[4,24,768]{2,1,0:T(8,128)(2,1)S(1)}, bf16[4,24,768]{2,1,0:T(8,128)(2,1)S(1)}, u32[]{:S(2)}, u32[]{:S(2)}) collective-permute-start(bf16[4,24,768]{2,1,0:T(8,128)(2,1)S(1)} %get-tuple-element.458), channel_id=1, source_target_pairs={{0,2},{1,3},{2,0},{3,1},{4,6},{5,7},{6,4},{7,5},{8,10},{9,11},{10,... | collective-permute-start | bytes 442376 | tf_op jit(solution)/shard_map/ppermute | solution.py:244
  29.1 22.3 %collective-permute-start.15 = (bf16[24,4096]{1,0:T(8,128)(2,1)S(1)}, bf16[24,4096]{1,0:T(8,128)(2,1)S(1)}, u32[]{:S(2)}, u32[]{:S(2)}) collective-permute-start(bf16[24,4096]{1,0:T(8,128)(2,1)S(1)} %copy-done.45), channel_id=1, source_target_pairs={{0,16},{1,17},{2,18},{3,19},{4,20},{5,21},{6,22},{7,23},{8,24},{9,... | collective-permute-start | bytes 589832 | tf_op jit(solution)/shard_map/ppermute | solution.py:244
  45.0 54.0 %collective-permute-start.49 = (bf16[2,48,4096]{2,1,0:T(8,128)(2,1)}, bf16[2,48,4096]{2,1,0:T(8,128)(2,1)S(1)}, u32[]{:S(2)}, u32[]{:S(2)}) collective-permute-start(bf16[2,48,4096]{2,1,0:T(8,128)(2,1)} %dynamic-slice_bitcast_fusion), channel_id=1, source_target_pairs={{0,1},{1,0},{2,3},{3,2},{4,5},{5,4},{6,7},{7,6},{8,9},{9,8},{10,11... | collective-permute-start | bytes 2359304 | tf_op jit(solution)/shard_map/ppermute | solution.py:244
  54.7 24.0 %collective-permute-start.3 = (bf16[4,24,2432]{2,1,0:T(8,128)(2,1)S(1)}, bf16[4,24,2432]{2,1,0:T(8,128)(2,1)S(1)}, u32[]{:S(2)}, u32[]{:S(2)}) collective-permute-start(bf16[4,24,2432]{2,1,0:T(8,128)(2,1)S(1)} %get-tuple-element.446), channel_id=1, source_target_pairs={{0,2},{1,3},{2,0},{3,1},{4,6},{5,7},{6,4},{7,5},{8,10},{9,11},{10,... | collective-permute-start | bytes 1400840 | tf_op jit(solution)/shard_map/ppermute | solution.py:244
  67.7 21.8 %collective-permute-start.5 = (bf16[4,24,2432]{2,1,0:T(8,128)(2,1)S(1)}, bf16[4,24,2432]{2,1,0:T(8,128)(2,1)S(1)}, u32[]{:S(2)}, u32[]{:S(2)}) collective-permute-start(bf16[4,24,2432]{2,1,0:T(8,128)(2,1)S(1)} %get-tuple-element.446), channel_id=1, source_target_pairs={{0,6},{1,7},{2,4},{3,5},{4,2},{5,3},{6,0},{7,1},{8,14},{9,15},{10,... | collective-permute-start | bytes 1400840 | tf_op jit(solution)/shard_map/ppermute | solution.py:244
  71.5 36.2 %collective-permute-start.13 = (bf16[4,4,24,768]{3,2,1,0:T(8,128)(2,1)S(1)}, bf16[4,4,24,768]{3,2,1,0:T(8,128)(2,1)S(1)}, u32[]{:S(2)}, u32[]{:S(2)}) collective-permute-start(bf16[4,4,24,768]{3,2,1,0:T(8,128)(2,1)S(1)} %get-tuple-element.441), channel_id=1, source_target_pairs={{0,1},{1,0},{2,3},{3,2},{4,5},{5,4},{6,7},{7,6},{8,9},{9,8},{10,11... | collective-permute-start | bytes 1769480 | tf_op jit(solution)/shard_map/ppermute | solution.py:244
  78.7 31.1 %collective-permute-start.17 = (bf16[4,24,4096]{2,1,0:T(8,128)(2,1)}, bf16[4,24,4096]{2,1,0:T(8,128)(2,1)}, u32[]{:S(2)}, u32[]{:S(2)}) collective-permute-start(bf16[4,24,4096]{2,1,0:T(8,128)(2,1)} %get-tuple-element.430), channel_id=1, source_target_pairs={{0,2},{1,3},{2,0},{3,1},{4,6},{5,7},{6,4},{7,5},{8,10},{9,11},{10,... | collective-permute-start | bytes 2359304 | tf_op jit(solution)/shard_map/ppermute | solution.py:244
  79.5 19.8 %collective-permute-start.56 = (bf16[128,768]{1,0:T(8,128)(2,1)S(1)}, bf16[128,768]{1,0:T(8,128)(2,1)S(1)}, u32[]{:S(2)}, u32[]{:S(2)}) collective-permute-start(bf16[128,768]{1,0:T(8,128)(2,1)S(1)} %get-tuple-element.434), channel_id=1, source_target_pairs={{0,4},{1,5},{2,6},{3,7},{4,0},{5,1},{6,2},{7,3},{8,12},{9,13},{10,... | collective-permute-start | bytes 589832 | tf_op jit(solution)/shard_map/ppermute | solution.py:244
  99.3 40.7 %collective-permute-start.18 = (bf16[4,24,4096]{2,1,0:T(8,128)(2,1)}, bf16[4,24,4096]{2,1,0:T(8,128)(2,1)}, u32[]{:S(2)}, u32[]{:S(2)}) collective-permute-start(bf16[4,24,4096]{2,1,0:T(8,128)(2,1)} %get-tuple-element.430), channel_id=1, source_target_pairs={{0,4},{1,5},{2,6},{3,7},{4,0},{5,1},{6,2},{7,3},{8,12},{9,13},{10,... | collective-permute-start | bytes 2359304 | tf_op jit(solution)/shard_map/ppermute | solution.py:244
  102.6 39.5 %collective-permute-start.19 = (bf16[4,24,4096]{2,1,0:T(8,128)(2,1)}, bf16[4,24,4096]{2,1,0:T(8,128)(2,1)}, u32[]{:S(2)}, u32[]{:S(2)}) collective-permute-start(bf16[4,24,4096]{2,1,0:T(8,128)(2,1)} %get-tuple-element.430), channel_id=1, source_target_pairs={{0,6},{1,7},{2,4},{3,5},{4,2},{5,3},{6,0},{7,1},{8,14},{9,15},{10,... | collective-permute-start | bytes 2359304 | tf_op jit(solution)/shard_map/ppermute | solution.py:244
  107.7 74.8 %collective-permute-start.27 = (bf16[4,4,64,768]{3,2,1,0:T(8,128)(2,1)S(1)}, bf16[4,4,64,768]{3,2,1,0:T(8,128)(2,1)}, u32[]{:S(2)}, u32[]{:S(2)}) collective-permute-start(bf16[4,4,64,768]{3,2,1,0:T(8,128)(2,1)S(1)} %pad_maximum_fusion.8), channel_id=1, source_target_pairs={{0,1},{1,0},{2,3},{3,2},{4,5},{5,4},{6,7},{7,6},{8,9},{9,8},{10,11... | collective-permute-start | bytes 4718600 | tf_op jit(solution)/shard_map/ppermute | solution.py:244
  107.7 78.2 %collective-permute-start.6 = (bf16[4,4,24,2432]{3,2,1,0:T(8,128)(2,1)}, bf16[4,4,24,2432]{3,2,1,0:T(8,128)(2,1)}, u32[]{:S(2)}, u32[]{:S(2)}) collective-permute-start(bf16[4,4,24,2432]{3,2,1,0:T(8,128)(2,1)} %get-tuple-element.348), channel_id=1, source_target_pairs={{0,1},{1,0},{2,3},{3,2},{4,5},{5,4},{6,7},{7,6},{8,9},{9,8},{10,11... | collective-permute-start | bytes 5603336 | tf_op jit(solution)/shard_map/ppermute | solution.py:244
  109.8 37.6 %collective-permute-start.50 = (bf16[48,4096]{1,0:T(8,128)(2,1)}, bf16[48,4096]{1,0:T(8,128)(2,1)}, u32[]{:S(2)}, u32[]{:S(2)}) collective-permute-start(bf16[48,4096]{1,0:T(8,128)(2,1)} %get-tuple-element.389), channel_id=1, source_target_pairs={{0,4},{1,5},{2,6},{3,7},{4,0},{5,1},{6,2},{7,3},{8,12},{9,13},{10,... | collective-permute-start | bytes 1179656 | tf_op jit(solution)/shard_map/ppermute | solution.py:244
  140.0 40.6 %collective-permute-start.59 = (bf16[4,128,768]{2,1,0:T(8,128)(2,1)S(1)}, bf16[4,128,768]{2,1,0:T(8,128)(2,1)S(1)}, u32[]{:S(2)}, u32[]{:S(2)}) collective-permute-start(bf16[4,128,768]{2,1,0:T(8,128)(2,1)S(1)} %get-tuple-element.432), channel_id=1, source_target_pairs={{0,16},{1,17},{2,18},{3,19},{4,20},{5,21},{6,22},{7,23},{8,24},{9,... | collective-permute-start | bytes 2359304 | tf_op jit(solution)/shard_map/ppermute | solution.py:244
  142.1 26.4 %collective-permute-start.51 = (bf16[48,4096]{1,0:T(8,128)(2,1)S(1)}, bf16[48,4096]{1,0:T(8,128)(2,1)S(1)}, u32[]{:S(2)}, u32[]{:S(2)}) collective-permute-start(bf16[48,4096]{1,0:T(8,128)(2,1)S(1)} %copy-done.44), channel_id=1, source_target_pairs={{0,8},{1,9},{2,10},{3,11},{4,12},{5,13},{6,14},{7,15},{8,0},{9,1},... | collective-permute-start | bytes 1179656 | tf_op jit(solution)/shard_map/ppermute | solution.py:244
  147.4 27.1 %collective-permute-start.52 = (bf16[48,4096]{1,0:T(8,128)(2,1)S(1)}, bf16[48,4096]{1,0:T(8,128)(2,1)S(1)}, u32[]{:S(2)}, u32[]{:S(2)}) collective-permute-start(bf16[48,4096]{1,0:T(8,128)(2,1)S(1)} %copy-done.43), channel_id=1, source_target_pairs={{0,12},{1,13},{2,14},{3,15},{4,8},{5,9},{6,10},{7,11},{8,4},{9,5},... | collective-permute-start | bytes 1179656 | tf_op jit(solution)/shard_map/ppermute | solution.py:244
  168.5 139.0 %collective-permute-start.20 = (bf16[4,4,24,4096]{3,2,1,0:T(8,128)(2,1)}, bf16[4,4,24,4096]{3,2,1,0:T(8,128)(2,1)}, u32[]{:S(2)}, u32[]{:S(2)}) collective-permute-start(bf16[4,4,24,4096]{3,2,1,0:T(8,128)(2,1)} %get-tuple-element.339), channel_id=1, source_target_pairs={{0,1},{1,0},{2,3},{3,2},{4,5},{5,4},{6,7},{7,6},{8,9},{9,8},{10,11... | collective-permute-start | bytes 9437192 | tf_op jit(solution)/shard_map/ppermute | solution.py:244
  177.3 125.0 %collective-permute-start.53 = (bf16[4,48,4096]{2,1,0:T(8,128)(2,1)}, bf16[4,48,4096]{2,1,0:T(8,128)(2,1)}, u32[]{:S(2)}, u32[]{:S(2)}) collective-permute-start(bf16[4,48,4096]{2,1,0:T(8,128)(2,1)} %get-tuple-element.387), channel_id=1, source_target_pairs={{0,16},{1,17},{2,18},{3,19},{4,20},{5,21},{6,22},{7,23},{8,24},{9,... | collective-permute-start | bytes 4718600 | tf_op jit(solution)/shard_map/ppermute | solution.py:244
  274.2 95.1 %collective-permute-start.60 = (bf16[2,4,128,768]{3,2,1,0:T(8,128)(2,1)}, bf16[2,4,128,768]{3,2,1,0:T(8,128)(2,1)}, u32[]{:S(2)}, u32[]{:S(2)}) collective-permute-start(bf16[2,4,128,768]{3,2,1,0:T(8,128)(2,1)} %get-tuple-element.385), channel_id=1, source_target_pairs={{0,1},{1,0},{2,3},{3,2},{4,5},{5,4},{6,7},{7,6},{8,9},{9,8},{10,11... | collective-permute-start | bytes 4718600 | tf_op jit(solution)/shard_map/ppermute | solution.py:244
  297.4 48.4 %collective-permute-start.28 = (bf16[128,768]{1,0:T(8,128)(2,1)}, bf16[128,768]{1,0:T(8,128)(2,1)}, u32[]{:S(2)}, u32[]{:S(2)}) collective-permute-start(bf16[128,768]{1,0:T(8,128)(2,1)} %get-tuple-element.406), channel_id=1, source_target_pairs={{0,2},{1,3},{2,0},{3,1},{4,6},{5,7},{6,4},{7,5},{8,10},{9,11},{10,... | collective-permute-start | bytes 589832 | tf_op jit(solution)/shard_map/ppermute | solution.py:244
  300.1 47.9 %collective-permute-start.29 = (bf16[128,768]{1,0:T(8,128)(2,1)}, bf16[128,768]{1,0:T(8,128)(2,1)}, u32[]{:S(2)}, u32[]{:S(2)}) collective-permute-start(bf16[128,768]{1,0:T(8,128)(2,1)} %get-tuple-element.405), channel_id=1, source_target_pairs={{0,4},{1,5},{2,6},{3,7},{4,0},{5,1},{6,2},{7,3},{8,12},{9,13},{10,... | collective-permute-start | bytes 589832 | tf_op jit(solution)/shard_map/ppermute | solution.py:244
  302.3 48.6 %collective-permute-start.30 = (bf16[128,768]{1,0:T(8,128)(2,1)}, bf16[128,768]{1,0:T(8,128)(2,1)}, u32[]{:S(2)}, u32[]{:S(2)}) collective-permute-start(bf16[128,768]{1,0:T(8,128)(2,1)} %get-tuple-element.404), channel_id=1, source_target_pairs={{0,6},{1,7},{2,4},{3,5},{4,2},{5,3},{6,0},{7,1},{8,14},{9,15},{10,... | collective-permute-start | bytes 589832 | tf_op jit(solution)/shard_map/ppermute | solution.py:244
  307.5 69.0 %collective-permute-start.54 = (bf16[2,4,48,4096]{3,2,1,0:T(8,128)(2,1)}, bf16[2,4,48,4096]{3,2,1,0:T(8,128)(2,1)}, u32[]{:S(2)}, u32[]{:S(2)}) collective-permute-start(bf16[2,4,48,4096]{3,2,1,0:T(8,128)(2,1)} %get-tuple-element.341), channel_id=1, source_target_pairs={{0,1},{1,0},{2,3},{3,2},{4,5},{5,4},{6,7},{7,6},{8,9},{9,8},{10,11... | collective-permute-start | bytes 9437192 | tf_op jit(solution)/shard_map/ppermute | solution.py:244
  345.8 28.9 %collective-permute-start.103 = (bf16[4,4,64,768]{3,2,1,0:T(8,128)(2,1)S(1)}, bf16[4,4,64,768]{3,2,1,0:T(8,128)(2,1)S(1)}, u32[]{:S(2)}, u32[]{:S(2)}) collective-permute-start(bf16[4,4,64,768]{3,2,1,0:T(8,128)(2,1)S(1)} %bitcast.500), channel_id=1, source_target_pairs={{0,1},{1,0},{2,3},{3,2},{4,5},{5,4},{6,7},{7,6},{8,9},{9,8},{10,11... | collective-permute-start | bytes 4718600 | tf_op jit(solution)/shard_map/ppermute | solution.py:244
  454.6 257.8 %collective-permute-start.96 = (bf16[4,4,2,24,2048]{4,3,1,2,0:T(8,128)(2,1)}, bf16[4,4,2,24,2048]{4,3,1,2,0:T(8,128)(2,1)}, u32[]{:S(2)}, u32[]{:S(2)}) collective-permute-start(bf16[4,4,2,24,2048]{4,3,1,2,0:T(8,128)(2,1)} %slice_bitcast_fusion), channel_id=1, source_target_pairs={{0,1},{1,0},{2,3},{3,2},{4,5},{5,4},{6,7},{7,6},{8,9},{9,8},{10,11... | collective-permute-start | bytes 9437192 | tf_op jit(solution)/shard_map/ppermute | solution.py:244
  454.6 216.7 %collective-permute-start.104 = (bf16[4,64,768]{2,1,0:T(8,128)(2,1)}, bf16[4,64,768]{2,1,0:T(8,128)(2,1)}, u32[]{:S(2)}, u32[]{:S(2)}) collective-permute-start(bf16[4,64,768]{2,1,0:T(8,128)(2,1)} %get-tuple-element.359), channel_id=1, source_target_pairs={{0,2},{1,3},{2,0},{3,1},{4,6},{5,7},{6,4},{7,5},{8,10},{9,11},{10,... | collective-permute-start | bytes 1179656 | tf_op jit(solution)/shard_map/ppermute | solution.py:244
  455.3 216.5 %collective-permute-start.105 = (bf16[4,64,768]{2,1,0:T(8,128)(2,1)}, bf16[4,64,768]{2,1,0:T(8,128)(2,1)}, u32[]{:S(2)}, u32[]{:S(2)}) collective-permute-start(bf16[4,64,768]{2,1,0:T(8,128)(2,1)} %get-tuple-element.361), channel_id=1, source_target_pairs={{0,4},{1,5},{2,6},{3,7},{4,0},{5,1},{6,2},{7,3},{8,12},{9,13},{10,... | collective-permute-start | bytes 1179656 | tf_op jit(solution)/shard_map/ppermute | solution.py:244
  490.6 143.4 %collective-permute-start.61 = (bf16[128,768]{1,0:T(8,128)(2,1)}, bf16[128,768]{1,0:T(8,128)(2,1)}, u32[]{:S(2)}, u32[]{:S(2)}) collective-permute-start(bf16[128,768]{1,0:T(8,128)(2,1)} %get-tuple-element.382), channel_id=1, source_target_pairs={{0,2},{1,3},{2,0},{3,1},{4,6},{5,7},{6,4},{7,5},{8,10},{9,11},{10,... | collective-permute-start | bytes 589832 | tf_op jit(solution)/shard_map/ppermute | solution.py:244
  494.3 141.5 %collective-permute-start.62 = (bf16[128,768]{1,0:T(8,128)(2,1)}, bf16[128,768]{1,0:T(8,128)(2,1)}, u32[]{:S(2)}, u32[]{:S(2)}) collective-permute-start(bf16[128,768]{1,0:T(8,128)(2,1)} %get-tuple-element.381), channel_id=1, source_target_pairs={{0,4},{1,5},{2,6},{3,7},{4,0},{5,1},{6,2},{7,3},{8,12},{9,13},{10,... | collective-permute-start | bytes 589832 | tf_op jit(solution)/shard_map/ppermute | solution.py:244
  648.7 23.1 %collective-permute-start.106 = (bf16[4,64,768]{2,1,0:T(8,128)(2,1)S(1)}, bf16[4,64,768]{2,1,0:T(8,128)(2,1)}, u32[]{:S(2)}, u32[]{:S(2)}) collective-permute-start(bf16[4,64,768]{2,1,0:T(8,128)(2,1)S(1)} %copy-done.42), channel_id=1, source_target_pairs={{0,6},{1,7},{2,4},{3,5},{4,2},{5,3},{6,0},{7,1},{8,14},{9,15},{10,... | collective-permute-start | bytes 1179656 | tf_op jit(solution)/shard_map/ppermute | solution.py:244
  659.6 59.1 %collective-permute-start.116 = (bf16[2,4,128,768]{3,2,1,0:T(8,128)(2,1)}, bf16[2,4,128,768]{3,2,1,0:T(8,128)(2,1)}, u32[]{:S(2)}, u32[]{:S(2)}) collective-permute-start(bf16[2,4,128,768]{3,2,1,0:T(8,128)(2,1)} %slice_bitcast_fusion.2), channel_id=1, source_target_pairs={{0,1},{1,0},{2,3},{3,2},{4,5},{5,4},{6,7},{7,6},{8,9},{9,8},{10,11... | collective-permute-start | bytes 4718600 | tf_op jit(solution)/shard_map/ppermute | solution.py:244
  707.1 51.3 %collective-permute-start.110 = (bf16[2,4,2,48,2048]{4,3,2,1,0:T(8,128)(2,1)}, bf16[2,4,2,48,2048]{4,3,2,1,0:T(8,128)(2,1)}, u32[]{:S(2)}, u32[]{:S(2)}) collective-permute-start(bf16[2,4,2,48,2048]{4,3,2,1,0:T(8,128)(2,1)} %bitcast.164), channel_id=1, source_target_pairs={{0,1},{1,0},{2,3},{3,2},{4,5},{5,4},{6,7},{7,6},{8,9},{9,8},{10,11... | collective-permute-start | bytes 9437192 | tf_op jit(solution)/shard_map/ppermute | solution.py:244
  716.8 20.5 %collective-permute-start.97 = (bf16[4,2,24,2048]{3,2,0,1:T(8,128)(2,1)S(1)}, bf16[4,2,24,2048]{3,2,0,1:T(8,128)(2,1)S(1)}, u32[]{:S(2)}, u32[]{:S(2)}) collective-permute-start(bf16[4,2,24,2048]{3,2,0,1:T(8,128)(2,1)S(1)} %get-tuple-element.335), channel_id=1, source_target_pairs={{0,2},{1,3},{2,0},{3,1},{4,6},{5,7},{6,4},{7,5},{8,10},{9,11},{10,... | collective-permute-start | bytes 2359304 | tf_op jit(solution)/shard_map/ppermute | solution.py:244
  716.9 34.0 %collective-permute-start.98 = (bf16[4,2,24,2048]{3,2,0,1:T(8,128)(2,1)S(1)}, bf16[4,2,24,2048]{3,2,0,1:T(8,128)(2,1)S(1)}, u32[]{:S(2)}, u32[]{:S(2)}) collective-permute-start(bf16[4,2,24,2048]{3,2,0,1:T(8,128)(2,1)S(1)} %get-tuple-element.337), channel_id=1, source_target_pairs={{0,4},{1,5},{2,6},{3,7},{4,0},{5,1},{6,2},{7,3},{8,12},{9,13},{10,... | collective-permute-start | bytes 2359304 | tf_op jit(solution)/shard_map/ppermute | solution.py:244
  718.7 36.7 %collective-permute-start.99 = (bf16[4,2,24,2048]{3,2,0,1:T(8,128)(2,1)S(1)}, bf16[4,2,24,2048]{3,2,0,1:T(8,128)(2,1)S(1)}, u32[]{:S(2)}, u32[]{:S(2)}) collective-permute-start(bf16[4,2,24,2048]{3,2,0,1:T(8,128)(2,1)S(1)} %get-tuple-element.336), channel_id=1, source_target_pairs={{0,6},{1,7},{2,4},{3,5},{4,2},{5,3},{6,0},{7,1},{8,14},{9,15},{10,... | collective-permute-start | bytes 2359304 | tf_op jit(solution)/shard_map/ppermute | solution.py:244
  722.3 41.6 %collective-permute-start.117 = (bf16[4,128,768]{2,1,0:T(8,128)(2,1)S(1)}, bf16[4,128,768]{2,1,0:T(8,128)(2,1)S(1)}, u32[]{:S(2)}, u32[]{:S(2)}) collective-permute-start(bf16[4,128,768]{2,1,0:T(8,128)(2,1)S(1)} %slice_bitcast_fusion.6), channel_id=1, source_target_pairs={{0,16},{1,17},{2,18},{3,19},{4,20},{5,21},{6,22},{7,23},{8,24},{9,... | collective-permute-start | bytes 2359304 | tf_op jit(solution)/shard_map/ppermute | solution.py:244
  737.3 70.7 %collective-permute-start.83 = (bf16[4,24,2432]{2,1,0:T(8,128)(2,1)S(1)}, bf16[4,24,2432]{2,1,0:T(8,128)(2,1)S(1)}, u32[]{:S(2)}, u32[]{:S(2)}) collective-permute-start(bf16[4,24,2432]{2,1,0:T(8,128)(2,1)S(1)} %get-tuple-element.344), channel_id=1, source_target_pairs={{0,2},{1,3},{2,0},{3,1},{4,6},{5,7},{6,4},{7,5},{8,10},{9,11},{10,... | collective-permute-start | bytes 1400840 | tf_op jit(solution)/shard_map/ppermute | solution.py:244
  757.1 48.0 %collective-permute-start.101 = (bf16[2,24,2048]{2,1,0:T(8,128)(2,1)S(1)}, bf16[2,24,2048]{2,1,0:T(8,128)(2,1)S(1)}, u32[]{:S(2)}, u32[]{:S(2)}) collective-permute-start(bf16[2,24,2048]{2,1,0:T(8,128)(2,1)S(1)} %get-tuple-element.428), channel_id=1, source_target_pairs={{0,16},{1,17},{2,18},{3,19},{4,20},{5,21},{6,22},{7,23},{8,24},{9,... | collective-permute-start | bytes 589832 | tf_op jit(solution)/shard_map/ppermute | solution.py:244
  758.4 47.1 %collective-permute-start.102 = (bf16[2,24,2048]{2,1,0:T(8,128)(2,1)S(1)}, bf16[2,24,2048]{2,1,0:T(8,128)(2,1)S(1)}, u32[]{:S(2)}, u32[]{:S(2)}) collective-permute-start(bf16[2,24,2048]{2,1,0:T(8,128)(2,1)S(1)} %get-tuple-element.427), channel_id=1, source_target_pairs={{0,24},{1,25},{2,26},{3,27},{4,28},{5,29},{6,30},{7,31},{8,16},{9,... | collective-permute-start | bytes 589832 | tf_op jit(solution)/shard_map/ppermute | solution.py:244
  763.9 78.1 %collective-permute-start.111 = (bf16[4,2,48,2048]{3,2,1,0:T(8,128)(2,1)S(1)}, bf16[4,2,48,2048]{3,2,1,0:T(8,128)(2,1)S(1)}, u32[]{:S(2)}, u32[]{:S(2)}) collective-permute-start(bf16[4,2,48,2048]{3,2,1,0:T(8,128)(2,1)S(1)} %slice_bitcast_fusion.4), channel_id=1, source_target_pairs={{0,16},{1,17},{2,18},{3,19},{4,20},{5,21},{6,22},{7,23},{8,24},{9,... | collective-permute-start | bytes 4718600 | tf_op jit(solution)/shard_map/ppermute | solution.py:244
  766.4 45.0 %collective-permute-start.84 = (bf16[4,24,2432]{2,1,0:T(8,128)(2,1)S(1)}, bf16[4,24,2432]{2,1,0:T(8,128)(2,1)S(1)}, u32[]{:S(2)}, u32[]{:S(2)}) collective-permute-start(bf16[4,24,2432]{2,1,0:T(8,128)(2,1)S(1)} %get-tuple-element.346), channel_id=1, source_target_pairs={{0,4},{1,5},{2,6},{3,7},{4,0},{5,1},{6,2},{7,3},{8,12},{9,13},{10,... | collective-permute-start | bytes 1400840 | tf_op jit(solution)/shard_map/ppermute | solution.py:244
  805.6 39.0 %collective-permute-start.118 = (bf16[128,768]{1,0:T(8,128)(2,1)S(1)}, bf16[128,768]{1,0:T(8,128)(2,1)S(1)}, u32[]{:S(2)}, u32[]{:S(2)}) collective-permute-start(bf16[128,768]{1,0:T(8,128)(2,1)S(1)} %get-tuple-element.425), channel_id=1, source_target_pairs={{0,4},{1,5},{2,6},{3,7},{4,0},{5,1},{6,2},{7,3},{8,12},{9,13},{10,... | collective-permute-start | bytes 589832 | tf_op jit(solution)/shard_map/ppermute | solution.py:244
  808.1 38.2 %collective-permute-start.119 = (bf16[128,768]{1,0:T(8,128)(2,1)S(1)}, bf16[128,768]{1,0:T(8,128)(2,1)S(1)}, u32[]{:S(2)}, u32[]{:S(2)}) collective-permute-start(bf16[128,768]{1,0:T(8,128)(2,1)S(1)} %get-tuple-element.424), channel_id=1, source_target_pairs={{0,8},{1,9},{2,10},{3,11},{4,12},{5,13},{6,14},{7,15},{8,0},{9,1},... | collective-permute-start | bytes 589832 | tf_op jit(solution)/shard_map/ppermute | solution.py:244
  811.4 40.2 %collective-permute-start.120 = (bf16[128,768]{1,0:T(8,128)(2,1)S(1)}, bf16[128,768]{1,0:T(8,128)(2,1)S(1)}, u32[]{:S(2)}, u32[]{:S(2)}) collective-permute-start(bf16[128,768]{1,0:T(8,128)(2,1)S(1)} %get-tuple-element.423), channel_id=1, source_target_pairs={{0,12},{1,13},{2,14},{3,15},{4,8},{5,9},{6,10},{7,11},{8,4},{9,5},... | collective-permute-start | bytes 589832 | tf_op jit(solution)/shard_map/ppermute | solution.py:244
  844.5 28.9 %collective-permute-start.114 = (bf16[2,48,2048]{2,1,0:T(8,128)(2,1)S(1)}, bf16[2,48,2048]{2,1,0:T(8,128)(2,1)S(1)}, u32[]{:S(2)}, u32[]{:S(2)}) collective-permute-start(bf16[2,48,2048]{2,1,0:T(8,128)(2,1)S(1)} %get-tuple-element.356), channel_id=1, source_target_pairs={{0,12},{1,13},{2,14},{3,15},{4,8},{5,9},{6,10},{7,11},{8,4},{9,5},... | collective-permute-start | bytes 1179656 | tf_op jit(solution)/shard_map/ppermute | solution.py:244
  846.3 28.4 %collective-permute-start.86 = (bf16[24,2432]{1,0:T(8,128)(2,1)S(1)}, bf16[24,2432]{1,0:T(8,128)(2,1)S(1)}, u32[]{:S(2)}, u32[]{:S(2)}) collective-permute-start(bf16[24,2432]{1,0:T(8,128)(2,1)S(1)} %get-tuple-element.442), channel_id=1, source_target_pairs={{0,8},{1,9},{2,10},{3,11},{4,12},{5,13},{6,14},{7,15},{8,0},{9,1},... | collective-permute-start | bytes 350216 | tf_op jit(solution)/shard_map/ppermute | solution.py:244
  851.6 23.1 %collective-permute-start.87 = (bf16[24,2432]{1,0:T(8,128)(2,1)S(1)}, bf16[24,2432]{1,0:T(8,128)(2,1)S(1)}, u32[]{:S(2)}, u32[]{:S(2)}) collective-permute-start(bf16[24,2432]{1,0:T(8,128)(2,1)S(1)} %get-tuple-element.444), channel_id=1, source_target_pairs={{0,16},{1,17},{2,18},{3,19},{4,20},{5,21},{6,22},{7,23},{8,24},{9,... | collective-permute-start | bytes 350216 | tf_op jit(solution)/shard_map/ppermute | solution.py:244
  (162 other events, 2107.1 us)

commit v2 on v1

v2 whole, which is shorter than its diff:
```python
import functools

import jax
import jax.numpy as jnp
from jax import lax
from jax.experimental import pallas as pl
from jax.experimental.pallas import tpu as pltpu
from jax.sharding import PartitionSpec as P

D = 768
HEADS = 12
HEAD_DIM = 64
FF = 2048
CHUNK = 256
PAIR = 2 * HEAD_DIM
SPAN = 256
BAND = 128
EXTRA = 16
AX = ("dp", "expert")
PAIR_LOW = True

epsilon = 1e-06
bf16 = jnp.bfloat16
f32 = jnp.float32


def dot(left, right, left_dim, right_dim, precision=None):
    return lax.dot_general(
        left,
        right,
        (((left_dim,), (right_dim,)), ((), ())),
        preferred_element_type=f32,
        precision=precision,
    )


def rope_tables(length):
    half_width = HEAD_DIM // 2
    frequency = 10000.0 ** (-jnp.arange(half_width, dtype=f32) / half_width)
    angles = jnp.arange(length, dtype=f32)[:, None] * frequency[None, :]
    return jnp.tile(jnp.cos(angles), (1, 4)), jnp.tile(jnp.sin(angles), (1, 4))


def swap_halves(values):
    first = lax.broadcasted_iota(jnp.int32, values.shape, 1) % HEAD_DIM < HEAD_DIM // 2
    up = pltpu.roll(values, PAIR - HEAD_DIM // 2, 1)
    down = pltpu.roll(values, HEAD_DIM // 2, 1)
    return up, down, first


def rotate(values, cosine, sine):
    up, down, first = swap_halves(values)
    return values * cosine + jnp.where(first, -up, down) * sine


def rotate_back(grads, cosine, sine):
    up, down, first = swap_halves(grads * sine)
    return grads * cosine + jnp.where(first, up, -down)


def norm_back(grad_normed, normed, scale):
    return scale * (grad_normed - normed * jnp.mean(grad_normed * normed, axis=-1, keepdims=True))


def unpermute(values, order):
    high = values.astype(bf16)
    rest = (values - high.astype(f32)).astype(bf16)
    return dot(high, order, 1, 1) + dot(rest, order, 1, 1)


def fill_bias(bias, column_ref, row_ref):
    length = bias.shape[0]
    query = lax.broadcasted_iota(jnp.int32, (length, length), 0)
    key = lax.broadcasted_iota(jnp.int32, (length, length), 1)
    allowed = (query >= key) & (column_ref[...] == row_ref[...])
    bias[...] = jnp.where(allowed, 0.0, -1000000000.0)


def bands(length):
    return [
        (slice(t, t + BAND), slice(max(0, t - SPAN), t + BAND)) for t in range(0, length, BAND)
    ]


def heads_of(values):
    lane = lax.broadcasted_iota(jnp.int32, values.shape, 1)
    zero = jnp.zeros_like(values)
    return jnp.where(lane < HEAD_DIM, values, zero), jnp.where(lane < HEAD_DIM, zero, values)


def attend_kernel(
    x_ref, wq_ref, wk_ref, wv_ref, cos_ref, sin_ref, column_ref, row_ref,
    q_ref, k_ref, v_ref, o_ref, lse_ref, bias,
):
    @pl.when(pl.program_id(0) == 0)
    def _():
        fill_bias(bias, column_ref, row_ref)

    x, cosine, sine = x_ref[...], cos_ref[...], sin_ref[...]
    query = rotate(dot(x, wq_ref[...], 1, 0), cosine, sine).astype(bf16)
    query = query * jnp.asarray(HEAD_DIM ** (-0.5), bf16)
    key = rotate(dot(x, wk_ref[...], 1, 0), cosine, sine).astype(bf16)
    value = dot(x, wv_ref[...], 1, 0).astype(bf16)
    q_ref[...], k_ref[...], v_ref[...] = query, key, value
    queries = heads_of(query)
    for rows, keys in bands(x.shape[0]):
        outs, totals = [], []
        for head in queries:
            scores = dot(head[rows], key[keys], 1, 1) + bias[rows, keys]
            top = jnp.max(scores, axis=-1, keepdims=True)
            weights = jnp.exp(scores - top)
            total = jnp.sum(weights, axis=-1, keepdims=True)
            probs = (weights * (1.0 / total)).astype(bf16)
            outs.append(dot(probs, value[keys], 1, 0))
            totals.append(jnp.broadcast_to(top + jnp.log(total), (BAND, PAIR)))
        lane = lax.broadcasted_iota(jnp.int32, (BAND, PAIR), 1)
        o_ref[rows, :] = jnp.where(lane < HEAD_DIM, outs[0], outs[1]).astype(bf16)
        lse_ref[rows, :] = jnp.where(lane < HEAD_DIM, totals[0], totals[1])


def attend(x, qkv, cosine, sine, column, row):
    length = x.shape[0]
    pairs = D // PAIR
    whole = lambda *shape: pl.BlockSpec(shape, lambda s: (0,) * len(shape))
    part = lambda n: pl.BlockSpec((D, PAIR), lambda s: (0, s + n * pairs))
    each = pl.BlockSpec((length, PAIR), lambda s: (0, s))
    return pl.pallas_call(
        attend_kernel,
        grid=(pairs,),
        in_specs=[
            whole(length, D), part(0), part(1), part(2), whole(length, PAIR),
            whole(length, PAIR), whole(length, 1), whole(1, length),
        ],
        out_specs=[each] * 5,
        out_shape=[jax.ShapeDtypeStruct((length, D), bf16)] * 4
        + [jax.ShapeDtypeStruct((length, D), f32)],
        scratch_shapes=[pltpu.VMEM((length, length), f32)],
        compiler_params=pltpu.CompilerParams(vmem_limit_bytes=40 << 20),
        cost_estimate=pl.CostEstimate(
            flops=20_000_000_000, bytes_accessed=10 * D * length + 6 * D * D, transcendentals=0
        ),
        name="attend",
    )(x, qkv, qkv, qkv, cosine, sine, column, row)


def attend_back_kernel(
    q_ref, k_ref, v_ref, lse_ref, grad_ref, x_ref, wq_ref, wk_ref, wv_ref, cos_ref, sin_ref,
    column_ref, row_ref, order_ref, tokens_ref, gain_ref, mid_ref,
    dw0_ref, dw1_ref, dx_ref, dgain_ref, bias, dq, dk, dv, normed_sum,
):
    step = pl.program_id(0)
    dw_refs = (dw0_ref, dw1_ref)

    @pl.when(step == 0)
    def _():
        fill_bias(bias, column_ref, row_ref)
        normed_sum[...] = jnp.zeros_like(normed_sum)

    key, value = k_ref[...], v_ref[...]
    queries, keys_of, grads = heads_of(q_ref[...]), heads_of(key), heads_of(grad_ref[...])
    dk[...] = jnp.zeros_like(dk)
    dv[...] = jnp.zeros_like(dv)
    for rows, keys in bands(key.shape[0]):
        query_sum = key_sum = value_sum = 0.0
        for n in range(2):
            head, grad = queries[n][rows], grads[n][rows]
            scores = dot(head, key[keys], 1, 1) + bias[rows, keys]
            probs = jnp.exp(scores - lse_ref[rows, n * HEAD_DIM : n * HEAD_DIM + 1])
            grad_probs = dot(grad, value[keys], 1, 1)
            shift = jnp.sum(grad_probs * probs, axis=-1, keepdims=True)
            low = (probs * (grad_probs - shift)).astype(bf16)
            value_sum += dot(probs.astype(bf16), grad, 0, 0)
            query_sum += dot(low, keys_of[n][keys], 1, 0)
            key_sum += dot(low, head, 0, 0)
        dq[rows, :] = query_sum * HEAD_DIM ** (-0.5)
        dk[keys, :] += key_sum
        dv[keys, :] += value_sum
    cosine, sine = cos_ref[...], sin_ref[...]
    parts = [
        rotate_back(dq[...], cosine, sine).astype(bf16),
        rotate_back(dk[...], cosine, sine).astype(bf16),
        dv[...].astype(bf16),
    ]
    x = x_ref[...]
    blocks, _, per, _ = dw_refs[0].shape
    for n, (part, weight_ref) in enumerate(zip(parts, (wq_ref, wk_ref, wv_ref), strict=True)):
        normed_sum[...] += dot(part, weight_ref[...], 1, 1)
        weight_grad = dot(x, part, 0, 0).astype(bf16)
        for i in range(2):
            for k in range(blocks):
                place = (i * blocks + k) * per
                dw_refs[i][k, n] = weight_grad[place : place + per]

    @pl.when(step == pl.num_programs(0) - 1)
    def _():
        stream = tokens_ref[...].astype(f32)
        scale = lax.rsqrt(jnp.mean(stream * stream, axis=-1, keepdims=True) + epsilon)
        normed = stream * scale
        grad_normed = unpermute(normed_sum[...], order_ref[...])
        dgain_ref[...] = jnp.sum(grad_normed * normed, axis=0, keepdims=True)
        dx_ref[...] = mid_ref[...] + norm_back(grad_normed * gain_ref[...], normed, scale)


def attend_back(
    query, key, value, lse, grad, x, qkv, cosine, sine, column, row, order, tokens, gain, mid, blocks
):
    length = x.shape[0]
    pairs = D // PAIR
    whole = lambda *shape: pl.BlockSpec(shape, lambda s: (0,) * len(shape))
    part = lambda n: pl.BlockSpec((D, PAIR), lambda s: (0, s + n * pairs))
    each = pl.BlockSpec((length, PAIR), lambda s: (0, s))
    return pl.pallas_call(
        attend_back_kernel,
        grid=(pairs,),
        in_specs=[
            each, each, each, each, each, whole(length, D), part(0), part(1), part(2),
            whole(length, PAIR), whole(length, PAIR), whole(length, 1), whole(1, length),
            whole(D, D), whole(length, D), whole(1, D), whole(length, D),
        ],
        out_specs=[
            pl.BlockSpec((blocks, 3, D // 2 // blocks, PAIR), lambda s: (0, 0, 0, s)),
            pl.BlockSpec((blocks, 3, D // 2 // blocks, PAIR), lambda s: (0, 0, 0, s)),
            whole(length, D),
            whole(1, D),
        ],
        out_shape=[
            jax.ShapeDtypeStruct((blocks, 3, D // 2 // blocks, D), bf16),
            jax.ShapeDtypeStruct((blocks, 3, D // 2 // blocks, D), bf16),
            jax.ShapeDtypeStruct((length, D), f32),
            jax.ShapeDtypeStruct((1, D), f32),
        ],
        scratch_shapes=[pltpu.VMEM((length, length), f32)]
        + [pltpu.VMEM((length, PAIR), f32)] * 3
        + [pltpu.VMEM((length, D), f32)],
        compiler_params=pltpu.CompilerParams(vmem_limit_bytes=48 << 20),
        cost_estimate=pl.CostEstimate(
            flops=40_000_000_000, bytes_accessed=20 * D * length + 12 * D * D, transcendentals=0
        ),
        name="attend_back",
    )(
        query, key, value, lse, grad, x, qkv, qkv, qkv, cosine, sine, column, row, order, tokens,
        gain, mid,
    )


def split_three(values, exact=False):
    parts = []
    for _ in range(3):
        high = lax.reduce_precision(values, 8, 7) if exact else values.astype(bf16).astype(f32)
        parts.append(high.astype(bf16))
        values = values - high
    return parts


def branch(x, u, gate_weight, up_weight, down):
    gate = dot(x, gate_weight, 1, 0)
    up = dot(x, up_weight, 1, 0)
    sigmoid = jax.nn.sigmoid(gate)
    act = gate * sigmoid
    slope = sigmoid * (1.0 + gate * (1.0 - sigmoid))
    grad_hidden = dot(u, down, 1, 1)
    hidden = (act * up).astype(bf16)
    return hidden, (grad_hidden * up * slope).astype(bf16), (grad_hidden * act).astype(bf16)


def accumulate(total, part):
    step = pl.program_id(0)

    @pl.when(step == 0)
    def _():
        total[...] = part

    @pl.when(step > 0)
    def _():
        total[...] += part


def shared_kernel(
    where_ref, a_ref, b_ref, x_ref, u_ref, order_ref, gate_ref, up_ref, *refs, cores, lanes
):
    down_refs, (out_ref, dx_ref), refs = refs[:cores], refs[cores : cores + 2], refs[cores + 2 :]
    dgu_refs, dd_refs, xp = refs[:cores], refs[cores : 2 * cores], refs[2 * cores]

    @pl.when(pl.program_id(0) == 0)
    def _():
        xp[...] = dot(x_ref[...], order_ref[...], 1, 0).astype(bf16)

    swap = where_ref[1] == 1
    slots = [lax.bitwise_xor(n, where_ref[0]) for n in range(lanes)]
    pieces = []
    for n in range(lanes):
        found = [r[0, slots[n], 0] for r in down_refs]
        if cores == 2:
            found = [jnp.where(swap, found[1], found[0]), jnp.where(swap, found[0], found[1])]
        pieces.extend(found)
    down = jnp.concatenate(pieces, axis=0)
    x, u = x_ref[...], u_ref[...]
    hidden, grad_gate, grad_up = branch(x, u, gate_ref[...], up_ref[...], down)
    accumulate(out_ref, dot(hidden, down, 1, 0))
    accumulate(dx_ref, dot(grad_gate, gate_ref[...], 1, 1) + dot(grad_up, up_ref[...], 1, 1))
    grad_down = dot(hidden, u, 0, 0).astype(bf16)
    per = grad_down.shape[0] // (cores * lanes)
    for n in range(lanes):
        found = [grad_down[(n * cores + i) * per : (n * cores + i + 1) * per] for i in range(cores)]
        if cores == 2:
            found = [jnp.where(swap, found[1], found[0]), jnp.where(swap, found[0], found[1])]
        for i in range(cores):
            dd_refs[i][0, slots[n], 0] = found[i]
    x = xp[...]
    blocks, _, per, _ = dgu_refs[0].shape
    for half, grads in ((0, grad_gate), (1, grad_up)):
        weight_grad = dot(x, grads, 0, 0).astype(bf16)
        for i in range(cores):
            for k in range(blocks):
                place = (i * blocks + k) * per
                dgu_refs[i][k, half] = weight_grad[place : place + per]


def whole(*shape):
    return pl.BlockSpec(shape, lambda *_: (0,) * len(shape))


def shared_branch(where, a_index, b_index, x, u, order, gate_up, downs, blocks):
    rows = x.shape[0]
    cores = len(downs)
    a_size, lanes, b_size, per_down, _ = downs[0].shape
    chunks = a_size * b_size
    width = FF // chunks
    per = D // cores // blocks
    down_spec = pl.BlockSpec((1, lanes, 1, per_down, D), lambda s, q, a, b: (a[s], 0, b[s], 0, 0))
    return pl.pallas_call(
        functools.partial(shared_kernel, cores=cores, lanes=lanes),
        grid_spec=pltpu.PrefetchScalarGridSpec(
            num_scalar_prefetch=3,
            grid=(chunks,),
            in_specs=[
                whole(rows, D),
                whole(rows, D),
                whole(D, D),
                pl.BlockSpec((D, width), lambda s, *_: (0, s)),
                pl.BlockSpec((D, width), lambda s, *_: (0, s + chunks)),
            ]
            + [down_spec] * cores,
            out_specs=[whole(rows, D)] * 2
            + [pl.BlockSpec((blocks, 2, per, width), lambda s, *_: (0, 0, 0, s))] * cores
            + [down_spec] * cores,
            scratch_shapes=[pltpu.VMEM((rows, D), bf16)],
        ),
        out_shape=[jax.ShapeDtypeStruct((rows, D), f32)] * 2
        + [jax.ShapeDtypeStruct((blocks, 2, per, FF), bf16)] * cores
        + [jax.ShapeDtypeStruct(downs[0].shape, bf16)] * cores,
        compiler_params=pltpu.CompilerParams(vmem_limit_bytes=48 << 20),
        cost_estimate=pl.CostEstimate(
            flops=2 * 9 * rows * D * FF, bytes_accessed=12 * D * FF, transcendentals=rows * FF
        ),
        name="shared_branch",
    )(where, a_index, b_index, x, u, order, gate_up, gate_up, *downs)


def expert_kernel(core_ref, columns_ref, x_ref, u_ref, w_ref, order_ref, *refs, cores, pairs, blocks):
    parts = cores * pairs
    gate_refs, up_refs, down_refs = (refs[i * parts : (i + 1) * parts] for i in range(3))
    out_ref, dx_ref = refs[3 * parts : 3 * parts + 2]
    refs = refs[3 * parts + 2 :]
    dgu_refs, dd_refs = refs[:parts], refs[parts : 2 * parts]
    xp, go, out_sum, dx_sum = refs[2 * parts :]
    step = pl.program_id(0)
    per_pair = pl.num_programs(0) // pairs

    owners, capacity = x_ref.shape[0], x_ref.shape[1] - EXTRA

    @pl.when(step == 0)
    def _():
        arrived = x_ref[:, :capacity, :].reshape(owners * capacity, D)
        xp[...] = dot(arrived, order_ref[...], 1, 0).astype(bf16)
        go[...] = (u_ref[...].astype(f32) * w_ref[...]).astype(bf16)

    def pick(values):
        chosen = values[0]
        for m in range(1, pairs):
            chosen = jnp.where(step >= m * per_pair, values[m], chosen)
        return chosen

    x, grad_out = xp[...], go[...]
    gate_weight = jnp.concatenate([r[...] for r in gate_refs], axis=0)
    up_weight = jnp.concatenate([r[...] for r in up_refs], axis=0)
    downs = [pick([down_refs[i * pairs + m][0] for m in range(pairs)]) for i in range(cores)]
    swap = core_ref[0] == 1
    if cores == 2:
        downs = [jnp.where(swap, downs[1], downs[0]), jnp.where(swap, downs[0], downs[1])]
    down = jnp.concatenate(downs, axis=0)
    hidden, grad_gate, grad_up = branch(x, grad_out, gate_weight, up_weight, down)
    accumulate(out_sum, dot(hidden, down, 1, 0))
    accumulate(dx_sum, dot(grad_gate, gate_weight, 1, 1) + dot(grad_up, up_weight, 1, 1))
    grad_down = dot(hidden, grad_out, 0, 0).astype(bf16)
    if cores == 2:
        half = grad_down.shape[0] // 2
        low, high = grad_down[:half], grad_down[half:]
        grad_downs = [jnp.where(swap, high, low), jnp.where(swap, low, high)]
    else:
        grad_downs = [grad_down]
    for m in range(pairs):

        @pl.when((step >= m * per_pair) & (step < (m + 1) * per_pair))
        def _(m=m):
            for i in range(cores):
                dd_refs[i * pairs + m][0] = grad_downs[i]

    for half, grads in ((0, grad_gate), (1, grad_up)):
        weight_grad = dot(x, grads, 0, 0).astype(bf16)
        per = D // parts // blocks
        for n in range(parts):
            for k in range(blocks):
                place = (n * blocks + k) * per
                dgu_refs[n][k, half] = weight_grad[place : place + per]

    @pl.when(step == pl.num_programs(0) - 1)
    def _():
        out_low = out_sum[...].astype(bf16)
        out_ref[...] = out_low
        grad_rows = dot(dx_sum[...].astype(bf16), order_ref[...], 1, 1).astype(bf16)
        product = u_ref[...].astype(f32) * out_low.astype(f32)
        grad_gates = dot(jnp.ones((8, D), f32), product, 1, 1, lax.Precision.HIGHEST)
        parts = split_three(grad_gates[0:1])
        blank = jnp.zeros((EXTRA - 3, capacity), bf16)
        for e in range(owners):
            dx_ref[e, :capacity] = grad_rows[e * capacity : (e + 1) * capacity]
            lanes = slice(e * capacity, (e + 1) * capacity)
            dx_ref[e, capacity:, :capacity] = jnp.concatenate([p[:, lanes] for p in parts] + [blank], axis=0)
            dx_ref[e, capacity:, capacity:] = jnp.zeros((EXTRA, D - capacity), bf16)


def expert_branch(core, columns, x, u, w, order, gate_ups, downs, cores, blocks):
    rows = u.shape[0]
    parts = len(gate_ups)
    pairs = parts // cores
    chunks = columns.shape[0]
    width = FF // chunks
    per_pair = chunks // pairs
    part_rows = D // parts
    per_down = width // cores

    def down_spec(m):
        place = lambda s, *_: (jnp.clip(s - m * per_pair, 0, per_pair - 1), 0, 0)
        return pl.BlockSpec((1, per_down, D), place)

    down_specs = [down_spec(n % pairs) for n in range(parts)]
    return pl.pallas_call(
        functools.partial(expert_kernel, cores=cores, pairs=pairs, blocks=blocks),
        grid_spec=pltpu.PrefetchScalarGridSpec(
            num_scalar_prefetch=2,
            grid=(chunks,),
            in_specs=[whole(*x.shape), whole(rows, D), whole(rows, 1), whole(D, D)]
            + [pl.BlockSpec((part_rows, width), lambda s, c, q: (0, q[s]))] * parts
            + [pl.BlockSpec((part_rows, width), lambda s, c, q: (0, q[s] + chunks))] * parts
            + down_specs,
            out_specs=[whole(rows, D), whole(*x.shape)]
            + [
                pl.BlockSpec(
                    (blocks, 2, part_rows // blocks, width), lambda s, c, q: (0, 0, 0, q[s])
                )
            ]
            * parts
            + down_specs,
            scratch_shapes=[
                pltpu.VMEM((rows, D), bf16),
                pltpu.VMEM((rows, D), bf16),
                pltpu.VMEM((rows, D), f32),
                pltpu.VMEM((rows, D), f32),
            ],
        ),
        out_shape=[
            jax.ShapeDtypeStruct((rows, D), bf16),
            jax.ShapeDtypeStruct(x.shape, bf16),
        ]
        + [jax.ShapeDtypeStruct((blocks, 2, part_rows // blocks, FF), bf16)] * parts
        + [jax.ShapeDtypeStruct((per_pair, per_down, D), bf16)] * parts,
        compiler_params=pltpu.CompilerParams(vmem_limit_bytes=56 << 20),
        cost_estimate=pl.CostEstimate(
            flops=2 * 9 * rows * D * FF,
            bytes_accessed=12 * D * FF + 12 * rows * D,
            transcendentals=rows * FF,
        ),
        name="expert_branch",
    )(core, columns, x, u, w, order, *gate_ups, *gate_ups, *downs)


def body(
    dp_size,
    expert_size,
    tokens,
    segment_ids,
    expert_ids,
    upstream,
    norm_first,
    qkv_weight,
    out_weight,
    norm_second,
    router_weight,
    shared_gate_up,
    shared_down,
    expert_gate_up,
    expert_down,
):
    devices = dp_size * expert_size
    lanes = expert_size // 2
    length = tokens.shape[0]
    experts = expert_gate_up.shape[0] * expert_size
    held = expert_gate_up.shape[0]
    group = experts // lanes
    pairs = dp_size // group
    capacity = length * 2 // experts
    tall = dp_size // 2

    me = lax.axis_index(AX).astype(jnp.int32)
    my_dp, my_expert = me // expert_size, me % expert_size
    my_x, my_c = my_expert // 2, my_expert % 2
    if PAIR_LOW:
        pair_of, group_of = (lambda d: d % pairs), (lambda d: d // pairs)
        dp_of = lambda p, g: g * pairs + p
    else:
        pair_of, group_of = (lambda d: d // group), (lambda d: d % group)
        dp_of = lambda p, g: p * group + g
    my_p, my_g = pair_of(my_dp), group_of(my_dp)

    def hop(values, offset):
        return lax.ppermute(values, AX, [(s, s ^ offset) for s in range(devices)])

    def arrive(values, offsets, after):
        blocks = [hop(v, o) for v, o in zip(values, offsets, strict=True)]
        if after:
            blocks = lax.optimization_barrier((blocks,) + after)[0]
        return blocks

    def spread(values, offsets, after=()):
        others = offsets[1:]
        return jnp.stack([values] + arrive([values] * len(others), others, after))

    def collect(blocks, offsets, after=()):
        others = offsets[1:]
        total = blocks[0].astype(f32)
        for block in arrive([blocks[i + 1] for i in range(len(others))], others, after):
            total = total + block.astype(f32)
        return total

    tall_offsets = [2 * i * expert_size for i in range(tall)]
    flat_offsets = [y * expert_size + 2 * x for y in range(2) for x in range(lanes)]
    pair_offsets = [dp_of(p, 0) * expert_size for p in range(pairs)]
    group_offsets = [dp_of(0, g) * expert_size for g in range(group)]

    def gate(values, *earlier):
        return lax.optimization_barrier((values,) + earlier)[0]

    def dense_home(position):
        i, j, c = position % tall, position // tall % (2 * lanes), position // tall // (2 * lanes)
        offset = (2 * i + j // lanes) * expert_size + 2 * (j % lanes) + c
        return lax.bitwise_xor(me, offset)

    def gather_expert(shard):
        halves = shard.reshape(held, 2, shard.shape[1] // 2, shard.shape[2])
        mine = lax.dynamic_index_in_dim(halves, my_c, 1, keepdims=False)
        other = hop(lax.dynamic_index_in_dim(halves, 1 - my_c, 1, keepdims=False), 1)
        all_held = jnp.concatenate(
            [jnp.where(my_c == 0, mine, other), jnp.where(my_c == 0, other, mine)], axis=0
        )
        parts = [
            lax.dynamic_index_in_dim(all_held, lax.bitwise_xor(my_g, g), 0, keepdims=False)
            for g in range(group)
        ]
        return parts

    def swap_groups(parts, after=()):
        blocks = arrive([parts[g] for g in range(1, group)], group_offsets[1:], after)
        return jnp.stack([parts[0]] + blocks)

    def settle_expert(parts):
        keep = [
            lax.dynamic_index_in_dim(parts, lax.bitwise_xor(my_g, my_c * held + j), 0)
            for j in range(held)
        ]
        give = [
            lax.dynamic_index_in_dim(parts, lax.bitwise_xor(my_g, (1 - my_c) * held + j), 0)
            for j in range(held)
        ]
        keep = jnp.concatenate(keep, axis=0)
        take = hop(jnp.concatenate(give, axis=0), 1)
        return jnp.stack([jnp.where(my_c == 0, keep, take), jnp.where(my_c == 0, take, keep)], axis=1)

    def expert_home(position):
        g, p, c = position % group, position // group % pairs, position // group // pairs
        dp = dp_of(lax.bitwise_xor(my_p, p), lax.bitwise_xor(my_g, g))
        return dp * 2 + lax.bitwise_xor(my_c, c)

    def order_of(home, blocks, width=D):
        per = width // blocks
        column = jnp.arange(width, dtype=jnp.int32)
        source = home(column // per) * per + column % per
        return (jnp.arange(width, dtype=jnp.int32)[:, None] == source[None, :]).astype(bf16)

    owners = [
        [dp_of(p, e % group) * expert_size + 2 * (e // group) + c for e in range(experts)]
        for p in range(pairs)
        for c in range(2)
    ]

    def exchange(rows):
        rows = rows.reshape((experts, -1, D))
        return lax.all_to_all(rows, AX, 0, 0, axis_index_groups=owners, tiled=True)

    dense_order = order_of(dense_home, devices)
    expert_order = order_of(expert_home, 2 * dp_size)

    def by_flat(grads):
        _, parts, _, width = grads.shape
        return jnp.swapaxes(grads.reshape(parts, 2 * lanes, -1, width), 0, 1)

    def by_tall(grads):
        parts, _, width = grads.shape
        return jnp.swapaxes(grads.reshape(parts, tall, -1, width), 0, 1)

    small = jnp.concatenate(
        [norm_first[:, None], norm_second[:, None], router_weight], axis=1
    )
    small = jnp.pad(small, ((0, 0), (0, 128 - small.shape[1])))
    qkv_full = spread(jnp.concatenate([qkv_weight, small, out_weight], axis=1), tall_offsets)
    gu_parts, down_parts = gather_expert(expert_gate_up), gather_expert(expert_down)
    qkv_full = spread(gate(qkv_full, gu_parts, down_parts), flat_offsets)
    expert_gu, expert_down = swap_groups(gu_parts), swap_groups(down_parts)
    shared_gu_full = lax.all_gather(shared_gate_up, AX, axis=0, tiled=True)
    shared_down_full = spread(gate(shared_down, gu_parts), tall_offsets)

    columns = jnp.arange(experts, dtype=jnp.int32)
    pickers = [(expert_ids[:, j : j + 1] == columns[None, :]).astype(f32) for j in range(2)]
    position = jnp.arange(length)
    earlier = (position[:, None] > position[None, :]).astype(bf16)
    counts = dot(earlier, (pickers[0] + pickers[1]).astype(bf16), 1, 0)
    kept, places = [], []
    for j in range(2):
        rank = jnp.sum(counts * pickers[j], axis=1).astype(jnp.int32)
        ids = expert_ids[:, j]
        kept_mask = rank < capacity
        slot = jnp.where(kept_mask, ids * capacity + rank, -1)
        kept.append(kept_mask.astype(f32))
        places.append(
            (slot[:, None] == jnp.arange(experts * capacity, dtype=jnp.int32)[None, :]).astype(bf16)
        )
    both_places = places[0] + places[1]

    def to_slots(values):
        return dot(both_places, values, 0, 0).astype(bf16)

    upstream_slots = to_slots(upstream)
    qkv_full = spread(gate(qkv_full, expert_gu, expert_down), [0, 1]).reshape(D, 4 * D + 128)
    out_full = qkv_full[:, 3 * D + 128 :]
    upstream_rows = exchange(gate(upstream_slots, qkv_full)).reshape(-1, D)

    small_full = dot(qkv_full[:, 3 * D : 3 * D + 128], dense_order, 0, 1)
    gain_one, gain_two = small_full[0:1], small_full[1:2]
    router_full = small_full[2 : 2 + experts].astype(bf16)
    stream = tokens.astype(f32)
    scale_one = lax.rsqrt(jnp.mean(stream * stream, axis=-1, keepdims=True) + epsilon)
    normed_one = stream * scale_one
    normed_low = (normed_one * gain_one).astype(bf16)
    normed_low = dot(normed_low, dense_order, 1, 0).astype(bf16)
    cosine, sine = rope_tables(length)
    column, row = segment_ids.reshape(length, 1), segment_ids
    ready = gate(normed_low, upstream_slots)
    query, key, value, attended, lse = attend(ready, qkv_full, cosine, sine, column, row)
    shared_down_full = spread(gate(shared_down_full, qkv_full), flat_offsets, (attended,))
    down_pairs = [expert_down] + arrive([expert_down] * (pairs - 1), pair_offsets[1:], (attended,))
    attended = gate(attended, upstream_rows, down_pairs, shared_down_full)
    attended = dot(attended, dense_order, 1, 0).astype(bf16)
    stream_mid = stream + dot(attended, out_full, 1, 0)
    scale_two = lax.rsqrt(jnp.mean(stream_mid * stream_mid, axis=-1, keepdims=True) + epsilon)
    normed_two = stream_mid * scale_two
    expert_in = (normed_two * gain_two).astype(bf16)
    logits = dot(expert_in, router_full, 1, 1)
    chosen = jnp.stack([jnp.sum(p * logits, axis=-1) for p in pickers], axis=1)
    chosen_top = jnp.max(chosen, axis=1, keepdims=True)
    chosen_exp = jnp.exp(chosen - chosen_top)
    gate_values = chosen_exp / jnp.sum(chosen_exp, axis=1, keepdims=True)
    kept_float = jnp.stack(kept, axis=1)
    mix_weight = kept_float * gate_values

    in_slots = to_slots(expert_in)
    slot_weight = sum(
        jnp.sum(places[j].astype(f32) * mix_weight[:, j : j + 1], axis=0) for j in range(2)
    )
    slot_weight = jnp.stack(split_three(slot_weight.reshape(experts, capacity), True), axis=1)
    slot_weight = jnp.pad(slot_weight, ((0, 0), (0, EXTRA - 3), (0, D - capacity)))
    in_slots = jnp.concatenate([in_slots.reshape(experts, capacity, D), slot_weight], axis=1)
    arrived = exchange(in_slots)
    slot_weight = jnp.sum(arrived[:, capacity : capacity + 3, :capacity].astype(f32), axis=1)
    slot_weight = slot_weight.reshape(experts * capacity, 1)
    relative = FF // dp_size == CHUNK
    dense_blocks = 2 * lanes if (D // (4 * lanes)) % 16 == 0 else 1
    shared_downs = [shared_down_full, hop(shared_down_full, 1)]
    if relative:
        shared_downs = [v.reshape(2, lanes, tall, -1, D) for v in shared_downs]
        place = jnp.arange(dp_size, dtype=jnp.int32)
        shared_a = lax.bitwise_xor(place % 2, my_dp % 2)
        shared_b = lax.bitwise_xor(place // 2, my_dp // 2)
        shared_where = jnp.stack([my_x, my_c])
    else:
        dense_rows = order_of(dense_home, devices, FF)
        shared_downs = jnp.stack(shared_downs).reshape(FF, D)
        shared_downs = dot(dense_rows, shared_downs, 1, 0).astype(bf16)
        shared_downs = [shared_downs.reshape(1, 1, -1, CHUNK, D)]
        shared_b = jnp.arange(FF // CHUNK, dtype=jnp.int32)
        shared_a = jnp.zeros_like(shared_b)
        shared_where = jnp.zeros((2,), jnp.int32)
    results = shared_branch(
        shared_where, shared_a, shared_b, gate(expert_in, in_slots), upstream, dense_order,
        shared_gu_full, shared_downs, dense_blocks if relative else 1,
    )
    shared_out, shared_dx = results[:2]
    if relative:
        shared_gu_grad, shared_down_grad = results[2:4], results[4:]
        if dense_blocks == 1:
            shared_gu_grad = [by_flat(g) for g in shared_gu_grad]
        shared_down_grad = [g.reshape(2 * lanes, -1, D) for g in shared_down_grad]
    else:
        shared_gu_grad = [by_flat(results[2][:, :, i * (D // 2) : (i + 1) * (D // 2)]) for i in range(2)]
        shared_down_grad = dot(dense_rows, results[3].reshape(FF, D), 0, 0).astype(bf16)
        shared_down_grad = list(shared_down_grad.reshape(2, 2 * lanes, -1, D))
    shared_gu_sum = collect(shared_gu_grad, [0, 1]).astype(bf16)
    shared_down_sum = collect(shared_down_grad, [0, 1]).astype(bf16)
    sent = (shared_gu_sum, shared_down_sum)
    upstream_rows = gate(upstream_rows, sent)

    gu_pairs = [expert_gu] + arrive(
        [gate(expert_gu, down_pairs)] * (pairs - 1), pair_offsets[1:], sent
    )
    gu_in = gu_pairs + [hop(v, 1) for v in gu_pairs]
    down_in = down_pairs + [hop(v, 1) for v in down_pairs]
    shards = 2 * pairs
    if relative:
        gu_in = [v.reshape(-1, 2 * FF) for v in gu_in]
        cores, blocks = 2, group
        place = jnp.arange(dp_size, dtype=jnp.int32)
        chunk_columns = dp_of(
            lax.bitwise_xor(place // group, my_p), lax.bitwise_xor(place % group, my_g)
        )
    else:
        expert_rows = order_of(expert_home, 2 * dp_size, FF)
        gu_in = [jnp.concatenate(gu_in, axis=0).reshape(D, 2 * FF)]
        down_in = jnp.concatenate(down_in, axis=0).reshape(FF, D)
        down_in = [dot(expert_rows, down_in, 1, 0).astype(bf16).reshape(-1, CHUNK, D)]
        cores, blocks = 1, 1
        chunk_columns = jnp.arange(FF // CHUNK, dtype=jnp.int32)
    results = expert_branch(
        my_c.reshape(1), chunk_columns, arrived, upstream_rows, slot_weight, expert_order, gu_in,
        down_in, cores, blocks,
    )
    expert_out, grad_rows = results[:2]
    gu_grads, down_grads = results[2 : 2 + len(gu_in)], results[2 + len(gu_in) :]
    if not relative:
        gu_grads = gu_grads[0].reshape(2, shards, group, -1, FF)
        gu_grads = [jnp.swapaxes(gu_grads[:, n], 0, 1) for n in range(shards)]
        down_grads = dot(expert_rows, down_grads[0].reshape(FF, D), 0, 0).astype(bf16)
        down_grads = [down_grads.reshape(shards, group, -1, D)[n] for n in range(shards)]

    shared_gu_sum = collect(shared_gu_sum, flat_offsets, (expert_out,)).astype(bf16)
    shared_down_sum = collect(shared_down_sum, flat_offsets, (expert_out,)).astype(bf16)
    buffer_rows = exchange(grad_rows)
    returned = exchange(gate(expert_out, buffer_rows)).reshape(-1, D)
    gu_sums = [collect(gu_grads[m::pairs], [0, 1]).astype(bf16) for m in range(pairs)]
    down_sums = [collect(down_grads[m::pairs], [0, 1]).astype(bf16) for m in range(pairs)]
    buffer_rows = gate(buffer_rows, gu_sums, down_sums, shared_gu_sum, shared_down_sum)
    gate_row = jnp.sum(buffer_rows[:, capacity : capacity + 3, :capacity].astype(f32), axis=1)
    buffer_rows = buffer_rows[:, :capacity].reshape(-1, D)

    cotangent = upstream.astype(f32)
    gate_row = gate_row.reshape(1, experts * capacity)
    grad_gate = jnp.stack(
        [jnp.sum(places[j].astype(f32) * gate_row, axis=1) for j in range(2)], axis=1
    )
    grad_chosen = gate_values * (
        grad_gate - jnp.sum(gate_values * grad_gate, axis=1, keepdims=True)
    )
    grad_logits = sum(pickers[j] * grad_chosen[:, j : j + 1] for j in range(2)).astype(bf16)
    router_grad = dot(grad_logits, expert_in, 0, 0)
    grad_expert_in = (
        shared_dx + dot(grad_logits, router_full, 1, 0) + dot(both_places, buffer_rows, 1, 0)
    )
    norm_second_grad = jnp.sum(grad_expert_in * normed_two, axis=0, keepdims=True)
    grad_mid = cotangent + norm_back(grad_expert_in * gain_two, normed_two, scale_two)
    grad_mid_low = grad_mid.astype(bf16)
    out_weight_grad = dot(attended, grad_mid_low, 0, 0)
    grad_attended = dot(grad_mid_low, out_full, 1, 1).astype(bf16)
    grad_attended = dot(grad_attended, dense_order, 1, 1).astype(bf16)
    out_weight_grad = out_weight_grad.astype(bf16).reshape(2, 2 * lanes, tall, -1, D)
    *qkv_grad, input_grad, norm_first_grad = attend_back(
        gate(query, out_weight_grad), key, value, lse, grad_attended, normed_low, qkv_full, cosine, sine, column, row,
        dense_order, tokens, gain_one, grad_mid, dense_blocks,
    )

    small_grad = jnp.concatenate([norm_first_grad, norm_second_grad, router_grad], axis=0)
    small_grad = jnp.swapaxes(small_grad.reshape(experts + 2, devices, D // devices), 0, 1)
    small_grad = gate(small_grad.reshape(devices, -1), returned)
    small_sum = jnp.sum(lax.all_to_all(small_grad, AX, 0, 0, tiled=True), axis=0)
    small_sum = small_sum.reshape(experts + 2, D // devices)

    if dense_blocks == 1:
        qkv_grad = [by_flat(g) for g in qkv_grad]
    done = (input_grad,)
    qkv_sum = collect(gate(qkv_grad, returned), [0, 1]).astype(bf16)
    out_sum = collect(out_weight_grad, [0, 1], done).astype(bf16)
    qkv_sum = collect(qkv_sum, flat_offsets).astype(bf16)
    out_sum = collect(out_sum, flat_offsets).astype(bf16)
    shared_gu_sum = collect(by_tall(shared_gu_sum), tall_offsets, done)
    shared_down_sum = collect(shared_down_sum.reshape(tall, -1, D), tall_offsets, done)
    mixed = stream_mid + shared_out
    for j in range(2):
        mixed = mixed + mix_weight[:, j : j + 1] * dot(places[j], returned, 1, 0)
    mixed = mixed.astype(bf16)
    expert_gu_sum = collect(gu_sums, pair_offsets, done).astype(bf16)
    expert_down_sum = collect(down_sums, pair_offsets, done).astype(bf16)
    expert_gu_sum = settle_expert(swap_groups(expert_gu_sum))
    expert_down_sum = settle_expert(swap_groups(expert_down_sum))
    out_sum = collect(out_sum, tall_offsets)
    qkv_sum = collect(gate(by_tall(qkv_sum), small_sum), tall_offsets)
    expert_gu_sum = jnp.moveaxis(expert_gu_sum, 2, 3).reshape(held, -1, 2 * FF).astype(f32)
    return (
        mixed,
        input_grad,
        small_sum[0],
        jnp.moveaxis(qkv_sum, 0, 1).reshape(-1, 3 * D),
        out_sum,
        small_sum[1],
        small_sum[2:].T,
        jnp.moveaxis(shared_gu_sum, 0, 1).reshape(-1, 2 * FF),
        shared_down_sum,
        expert_gu_sum,
        expert_down_sum.reshape(held, -1, D).astype(f32),
    )


def solution(mesh):
    rows = P(AX, None)
    split = P("expert", "dp", None)
    in_specs = (rows,) * 4 + (P(AX), rows, rows, P(AX)) + (rows,) * 3 + (split,) * 2
    out_specs = (rows, rows, P(AX), rows, rows, P(AX)) + (rows,) * 3 + (split,) * 2
    inner = functools.partial(body, mesh.shape["dp"], mesh.shape["expert"])
    return jax.shard_map(inner, mesh=mesh, in_specs=in_specs, out_specs=out_specs, check_vma=False)
```

time: 894 us -> 610 us (0.68)
  matrix products: 165 us -> 23.3 us
  waiting for transfers between devices: 282 us -> 170 us
  local copies, waits for them, and re-layouts: 110 us -> 38.6 us
  Pallas kernels: 81.3 us -> 137 us
  other arithmetic: 88.5 us -> 65.6 us
  between operations: 2.5 us -> 15.9 us
    ppermute x122 -> x70, waiting for transfers between devices: 282 us -> 126 us  [hop(): return lax.ppermute(values, AX, [(s, s ^ offset) for s in range(devices)])]
    dot_general x108 -> x15, matrix products: 165 us -> 23.3 us  [dot(): lax.dot_general(left, right, (((left_dim,), (right_dim,)), ((), ())), pre...]
    pallas_call x2 -> x4, Pallas kernels: 81.3 us -> 137 us  [the longest x1 58.4 us: expert_branch(): pl.pallas_call(functools.partial(expert_kernel, cores=cores, pairs=pairs,...]
    all_to_all x0 -> x5, waiting for transfers between devices: none -> 44.1 us  [the longest x4 28.2 us: exchange(): return lax.all_to_all(rows, AX, 0, 0, axis_index_groups=owners, tiled=True)]
    ppermute x122 -> x70, starting transfers between devices: 155 us -> 129 us  [hop(): return lax.ppermute(values, AX, [(s, s ^ offset) for s in range(devices)])]
    unnamed x206 -> x178, local copies, waits for them, and re-layouts: 34.5 us -> 10.6 us
    all_to_all x0 -> x5, starting transfers between devices: none -> 23.9 us  [the longest x4 19.9 us: exchange(): return lax.all_to_all(rows, AX, 0, 0, axis_index_groups=owners, tiled=True)]
    another operation x28 -> x13, other arithmetic: 37 us -> 17.8 us  [the longest x6 12.7 us: spread(): return jnp.stack([values] + arrive([values] * len(others), others, after))]
  transfers between devices with their start and end apart: 122 -> 76, of which waited for: 51 -> 24; matrix products, arithmetic and copies ran while one was open for 38% -> 19% of each run, Pallas kernels for 3% -> 18%
where the time goes in v2:
time: 610 us; the launch traced here: 603 us
  waiting for transfers between devices  170 us (28%)
  starting transfers between devices  153 us (25%)
  Pallas kernels  137 us (22%)
  other arithmetic  65.6 us (11%)
  local copies, waits for them, and re-layouts  38.6 us (6%)
  matrix products  23.3 us (4%)
  between operations  15.9 us (3%)
    ppermute x70, starting transfers between devices, hop(): return lax.ppermute(values, AX, [(s, s ^ offset) for s in range(devices)])  129 us
    ppermute x70, waiting for transfers between devices, hop(): return lax.ppermute(values, AX, [(s, s ^ offset) for s in range(devices)])  126 us
    pallas_call x1, Pallas kernels, expert_branch(): pl.pallas_call(functools.partial(expert_kernel, cores=cores, pairs=pairs,...  58.4 us
    pallas_call x1, Pallas kernels, shared_branch(): pl.pallas_call(functools.partial(shared_kernel, cores=cores, lanes=lanes)...  28.6 us
    all_to_all x4, waiting for transfers between devices, exchange(): return lax.all_to_all(rows, AX, 0, 0, axis_index_groups=owners, tiled=True)  28.2 us
    pallas_call x1, Pallas kernels, attend_back(): pl.pallas_call(attend_back_kernel, grid=(pairs,), in_specs=[each, each, e...  26.8 us
    dot_general x15, matrix products, dot(): lax.dot_general(left, right, (((left_dim,), (right_dim,)), ((), ())), pre...  23.3 us
    pallas_call x1, Pallas kernels, attend(): pl.pallas_call(attend_kernel, grid=(pairs,), in_specs=[whole(length, D),...  23 us
  transfers between devices with their start and end apart: 76, of which 24 were waited for; matrix products, arithmetic and copies ran while one was open for 19% of the time, Pallas kernels for 18%

profile of v2, /device:TPU:0, one launch (start us, length us, event | category | flops | bytes accessed | tf_op | source)
XLA Modules:
  0.0 603.1 jit_solution(14484009782295749778)
XLA Ops:
  9.7 3.0 collective-permute-start
  20.8 3.5 collective-permute-start.12
  27.5 15.7 %collective-permute-start.9 = (bf16[48,4096]{1,0:T(8,128)(2,1)S(1)}, bf16[48,4096]{1,0:T(8,128)(2,1)S(1)}, u32[]{:S(2)}, u32[]{:S(2)}) collective-permute-start(bf16[48,4096]{1,0:T(8,128)(2,1)S(1)} %get-tuple-element.170), channel_id=1, source_target_pairs={{0,16},{1,17},{2,18},{3,19},{4,20},{5,21},{6,22},{7,23},{8,24},{9,... | collective-permute-start | bytes 1179656 | tf_op jit(solution)/shard_map/ppermute | solution.py:527
  44.3 3.2 collective-permute-done.12
  56.0 29.5 %collective-permute-done.9 = bf16[48,4096]{1,0:T(8,128)(2,1)S(1)} collective-permute-done((bf16[48,4096]{1,0:T(8,128)(2,1)S(1)}, bf16[48,4096]{1,0:T(8,128)(2,1)S(1)}, u32[]{:S(2)}, u32[]{:S(2)}) %collective-permute-start.9) | collective-permute-done | bytes 393248 | tf_op jit(solution)/shard_map/ppermute | solution.py:527
  94.4 12.4 %collective-permute-start.16 = (bf16[64,768]{1,0:T(8,128)(2,1)S(1)}, bf16[64,768]{1,0:T(8,128)(2,1)S(1)}, u32[]{:S(2)}, u32[]{:S(2)}) collective-permute-start(bf16[64,768]{1,0:T(8,128)(2,1)S(1)} %copy-done.55), channel_id=1, source_target_pairs={{0,8},{1,9},{2,10},{3,11},{4,12},{5,13},{6,14},{7,15},{8,0},{9,1},... | collective-permute-start | bytes 294920 | tf_op jit(solution)/shard_map/ppermute | solution.py:527
  106.9 2.9 collective-permute-start.17
  115.1 4.1 collective-permute-done.18
  120.0 5.1 pad_maximum_fusion
  128.6 6.0 %all-to-all-start = ((bf16[8,128,768]{2,1,0:T(8,128)(2,1)}), bf16[8,128,768]{2,1,0:T(8,128)(2,1)}, u32[]{:S(2)}, u32[]{:S(2)}) async-start(bf16[8,128,768]{2,1,0:T(8,128)(2,1)} %bitcast.260), calls=%async_computation | async-start | bytes 3145728 | tf_op jit(solution)/shard_map/all_to_all | solution.py:608
  138.1 23.0 %attend.1 = (bf16[512,768]{1,0:T(8,128)(2,1)S(1)}, bf16[512,768]{1,0:T(8,128)(2,1)S(1)}, bf16[512,768]{1,0:T(8,128)(2,1)S(1)}, bf16[512,768]{1,0:T(8,128)(2,1)S(1)}, f32[512,768]{1,0:T(8,128)S(1)}) custom-call(bf16[512,768]{1,0:T(8,128)(2,1)S(1)} %fusion.22.x_ref, bf16[768,3200]{1,0:T(8,128)(2,1)S(1)} %bitcast.244, bf16[768,3200]{1,0:T(8,128)(2,1)S(1)} %bitcast.245, ...), custom_call_target="tpu_custom_call" | custom-call | flops 20000000000 | bytes 7471104 | tf_op jit(solution)/shard_map/attend/pallas_call | solution.py:127
  162.1 3.9 pad_maximum_fusion.4
  166.1 5.5 all-to-all-done
  183.0 28.6 %shared_branch.1 = (f32[512,768]{1,0:T(8,128)S(1)}, f32[512,768]{1,0:T(8,128)S(1)}, bf16[4,2,96,2048]{3,2,1,0:T(8,128)(2,1)}, bf16[4,2,96,2048]{3,2,1,0:T(8,128)...) custom-call(s32[2]{0:T(128)S(1)} %copy-done.16, s32[8]{0:T(128)S(1)} %get-tuple-element.222.a_ref, ...), custom_call_target="tpu_custom_call" | custom-call | flops 14495514624 | bytes 18874368 | tf_op jit(solution)/shard_map/shared_branch/pallas_call | solution.py:331
  213.2 4.5 all-to-all-start.1
  221.0 3.6 fusion
  224.6 4.9 add_convert_fusion
  229.5 24.9 %collective-permute-done.25 = bf16[4,48,4096]{2,1,0:T(8,128)(2,1)} collective-permute-done((bf16[4,48,4096]{2,1,0:T(8,128)(2,1)}, bf16[4,48,4096]{2,1,0:T(8,128)(2,1)}, u32[]{:S(2)}, u32[]{:S(2)}) %collective-permute-start.25) | collective-permute-done | bytes 1572896 | tf_op jit(solution)/shard_map/ppermute | solution.py:527
  256.9 3.3 all-to-all-done.1.x_ref
  264.8 3.0 slice_bitcast_fusion
  271.3 58.4 %expert_branch.1 = (bf16[1024,768]{1,0:T(8,128)(2,1)}, bf16[8,144,768]{2,1,0:T(8,128)(2,1)}, bf16[4,2,48,2048]{3,2,1,0:T(8,128)(2,1)}, bf16[4,2,48,2048]{3,2,1,0...) custom-call(s32[1]{0:T(128)} %bitcast.52.core_ref, ...), custom_call_target="tpu_custom_call" | custom-call | flops 28991029248 | bytes 28311552 | tf_op jit(solution)/shard_map/expert_branch/pallas_call | solution.py:448
  329.7 4.5 all-to-all-start.2
  337.8 8.2 %collective-permute-done.38 = bf16[256,768]{1,0:T(8,128)(2,1)} collective-permute-done((bf16[256,768]{1,0:T(8,128)(2,1)}, bf16[256,768]{1,0:T(8,128)(2,1)}, u32[]{:S(2)}, u32[]{:S(2)}) %collective-permute-start.38) | collective-permute-done | bytes 393248 | tf_op jit(solution)/shard_map/ppermute | solution.py:527
  346.0 8.2 %collective-permute-done.39 = bf16[256,768]{1,0:T(8,128)(2,1)} collective-permute-done((bf16[256,768]{1,0:T(8,128)(2,1)S(1)}, bf16[256,768]{1,0:T(8,128)(2,1)}, u32[]{:S(2)}, u32[]{:S(2)}) %collective-permute-start.39) | collective-permute-done | bytes 393248 | tf_op jit(solution)/shard_map/ppermute | solution.py:527
  357.6 10.0 %collective-permute-start.57 = (bf16[64,768]{1,0:T(8,128)(2,1)}, bf16[64,768]{1,0:T(8,128)(2,1)}, u32[]{:S(2)}, u32[]{:S(2)}) collective-permute-start(bf16[64,768]{1,0:T(8,128)(2,1)} %get-tuple-element.200), channel_id=1, source_target_pairs={{0,8},{1,9},{2,10},{3,11},{4,12},{5,13},{6,14},{7,15},{8,0},{9,1},... | collective-permute-start | bytes 294920 | tf_op jit(solution)/shard_map/ppermute | solution.py:527
  370.7 3.3 collective-permute-start.58
  378.8 4.9 all-to-all-start.3
  383.7 3.0 collective-permute-start.60
  386.7 3.7 add_convert_fusion.4
  390.4 2.7 slice.222
  401.6 19.3 %all-to-all-done.3 = bf16[8,128,768]{2,1,0:T(8,128)(2,1)} async-done(((bf16[8,128,768]{2,1,0:T(8,128)(2,1)}), bf16[8,128,768]{2,1,0:T(8,128)(2,1)}, u32[]{:S(2)}, u32[]{:S(2)}) %all-to-all-start.3) | async-done | bytes 1572896 | tf_op jit(solution)/shard_map/all_to_all | solution.py:608
  428.6 3.5 fusion.24.grad_ref
  435.5 26.8 %attend_back.1 = (bf16[4,3,96,768]{3,2,1,0:T(8,128)(2,1)}, bf16[4,3,96,768]{3,2,1,0:T(8,128)(2,1)}, f32[512,768]{1,0:T(8,128)}, f32[1,768]{1,0:T(1,128)S(1)}) custom-call(bf16[512,768]{1,0:T(8,128)(2,1)S(1)} %copy-done.21, bf16[512,768]{1,0:T(8,128)(2,1)S(1)} %copy-done.23, bf16[512,768]{1,0:T(8,128)(2,1)S(1)} %copy-done.25, f32[512,768]{1,0:T(8,128)} %copy-done.19, ...), custom_call_target="tpu_custom_call" | custom-call | flops 40000000000 | bytes 14942208 | tf_op jit(solution)/shard_map/attend_back/pallas_call | solution.py:212
  467.8 4.1 collective-permute-start.56
  473.5 3.8 collective-permute-start.68
  477.3 2.9 collective-permute-done.55
  481.1 12.8 %collective-permute-start.62 = (bf16[2,48,2048]{2,1,0:T(8,128)(2,1)S(1)}, bf16[2,48,2048]{2,1,0:T(8,128)(2,1)}, u32[]{:S(2)}, u32[]{:S(2)}) collective-permute-start(bf16[2,48,2048]{2,1,0:T(8,128)(2,1)S(1)} %get-tuple-element.160), channel_id=1, source_target_pairs={{0,16},{1,17},{2,18},{3,19},{4,20},{5,21},{6,22},{7,23},{8,24},{9,... | collective-permute-start | bytes 1179656 | tf_op jit(solution)/shard_map/ppermute | solution.py:527
  495.0 4.0 all-to-all-start.4
  502.7 15.9 %all-to-all-done.4 = f32[32,1,240]{2,1,0:T(1,128)S(1)} async-done(((f32[32,1,240]{2,1,0:T(1,128)}), f32[32,1,240]{2,1,0:T(1,128)S(1)}, u32[]{:S(2)}, u32[]{:S(2)}) %all-to-all-start.4) | async-done | bytes 30752 | tf_op jit(solution)/shard_map/all_to_all | solution.py:801
  518.7 2.9 collective-permute-start.63
  524.9 6.5 %collective-permute-done.63 = bf16[2,48,2048]{2,1,0:T(8,128)(2,1)S(1)} collective-permute-done((bf16[2,48,2048]{2,1,0:T(8,128)(2,1)S(1)}, bf16[2,48,2048]{2,1,0:T(8,128)(2,1)S(1)}, u32[]{:S(2)}, u32[]{:S(2)}) %collective-permute-start.63) | collective-permute-done | bytes 393248 | tf_op jit(solution)/shard_map/ppermute | solution.py:527
  536.8 3.1 collective-permute-done.48
  539.9 3.7 collective-permute-done.49
  543.7 7.2 %collective-permute-start.51 = (bf16[24,768]{1,0:T(8,128)(2,1)S(1)}, bf16[24,768]{1,0:T(8,128)(2,1)S(1)}, u32[]{:S(2)}, u32[]{:S(2)}) collective-permute-start(bf16[24,768]{1,0:T(8,128)(2,1)S(1)} %get-tuple-element.202), channel_id=1, source_target_pairs={{0,8},{1,9},{2,10},{3,11},{4,12},{5,13},{6,14},{7,15},{8,0},{9,1},... | collective-permute-start | bytes 110600 | tf_op jit(solution)/shard_map/ppermute | solution.py:527
  562.6 9.5 %collective-permute-done.41 = bf16[3,96,768]{2,1,0:T(8,128)(2,1)S(1)} collective-permute-done((bf16[3,96,768]{2,1,0:T(8,128)(2,1)S(1)}, bf16[3,96,768]{2,1,0:T(8,128)(2,1)S(1)}, u32[]{:S(2)}, u32[]{:S(2)}) %collective-permute-start.41) | collective-permute-done | bytes 442400 | tf_op jit(solution)/shard_map/ppermute | solution.py:527
  572.1 7.9 %collective-permute-done.42 = bf16[3,96,768]{2,1,0:T(8,128)(2,1)S(1)} collective-permute-done((bf16[3,96,768]{2,1,0:T(8,128)(2,1)S(1)}, bf16[3,96,768]{2,1,0:T(8,128)(2,1)S(1)}, u32[]{:S(2)}, u32[]{:S(2)}) %collective-permute-start.42) | collective-permute-done | bytes 442400 | tf_op jit(solution)/shard_map/ppermute | solution.py:527
  583.3 2.7 collective-permute-start.46
  588.7 3.8 reshape.553
  (418 shorter events, 149.3 us)
Async XLA Ops:
  7.2 174.0 %all-gather.2.cloned.1.call-start = ((), (), s32[]{:S(2)}) async-start(), calls=%async_computation.5 | async-start | bytes 6488064 | tf_op jit(solution)/shard_map/all_gather | solution.py:629
  19.8 23.4 %collective-permute-start.11 = (bf16[128,768]{1,0:T(8,128)(2,1)S(1)}, bf16[128,768]{1,0:T(8,128)(2,1)S(1)}, u32[]{:S(2)}, u32[]{:S(2)}) collective-permute-start(bf16[128,768]{1,0:T(8,128)(2,1)S(1)} %get-tuple-element.189), channel_id=1, source_target_pairs={{0,8},{1,9},{2,10},{3,11},{4,12},{5,13},{6,14},{7,15},{8,0},{9,1},... | collective-permute-start | bytes 589832 | tf_op jit(solution)/shard_map/ppermute | solution.py:527
  20.8 26.7 %collective-permute-start.12 = (bf16[128,768]{1,0:T(8,128)(2,1)S(1)}, bf16[128,768]{1,0:T(8,128)(2,1)S(1)}, u32[]{:S(2)}, u32[]{:S(2)}) collective-permute-start(bf16[128,768]{1,0:T(8,128)(2,1)S(1)} %get-tuple-element.190), channel_id=1, source_target_pairs={{0,16},{1,17},{2,18},{3,19},{4,20},{5,21},{6,22},{7,23},{8,24},{9,... | collective-permute-start | bytes 589832 | tf_op jit(solution)/shard_map/ppermute | solution.py:527
  25.0 24.0 %collective-permute-start.13 = (bf16[128,768]{1,0:T(8,128)(2,1)S(1)}, bf16[128,768]{1,0:T(8,128)(2,1)S(1)}, u32[]{:S(2)}, u32[]{:S(2)}) collective-permute-start(bf16[128,768]{1,0:T(8,128)(2,1)S(1)} %get-tuple-element.191), channel_id=1, source_target_pairs={{0,24},{1,25},{2,26},{3,27},{4,28},{5,29},{6,30},{7,31},{8,16},{9,... | collective-permute-start | bytes 589832 | tf_op jit(solution)/shard_map/ppermute | solution.py:527
  27.5 25.0 %collective-permute-start.8 = (bf16[48,4096]{1,0:T(8,128)(2,1)S(1)}, bf16[48,4096]{1,0:T(8,128)(2,1)S(1)}, u32[]{:S(2)}, u32[]{:S(2)}) collective-permute-start(bf16[48,4096]{1,0:T(8,128)(2,1)S(1)} %get-tuple-element.169), channel_id=1, source_target_pairs={{0,8},{1,9},{2,10},{3,11},{4,12},{5,13},{6,14},{7,15},{8,0},{9,1},... | collective-permute-start | bytes 1179656 | tf_op jit(solution)/shard_map/ppermute | solution.py:527
  27.5 58.0 %collective-permute-start.9 = (bf16[48,4096]{1,0:T(8,128)(2,1)S(1)}, bf16[48,4096]{1,0:T(8,128)(2,1)S(1)}, u32[]{:S(2)}, u32[]{:S(2)}) collective-permute-start(bf16[48,4096]{1,0:T(8,128)(2,1)S(1)} %get-tuple-element.170), channel_id=1, source_target_pairs={{0,16},{1,17},{2,18},{3,19},{4,20},{5,21},{6,22},{7,23},{8,24},{9,... | collective-permute-start | bytes 1179656 | tf_op jit(solution)/shard_map/ppermute | solution.py:527
  43.2 42.2 %collective-permute-start.10 = (bf16[48,4096]{1,0:T(8,128)(2,1)S(1)}, bf16[48,4096]{1,0:T(8,128)(2,1)S(1)}, u32[]{:S(2)}, u32[]{:S(2)}) collective-permute-start(bf16[48,4096]{1,0:T(8,128)(2,1)S(1)} %get-tuple-element.167), channel_id=1, source_target_pairs={{0,24},{1,25},{2,26},{3,27},{4,28},{5,29},{6,30},{7,31},{8,16},{9,... | collective-permute-start | bytes 1179656 | tf_op jit(solution)/shard_map/ppermute | solution.py:527
  47.6 39.3 %collective-permute-start.5 = (bf16[4,24,3200]{2,1,0:T(8,128)(2,1)S(1)}, bf16[4,24,3200]{2,1,0:T(8,128)(2,1)S(1)}, u32[]{:S(2)}, u32[]{:S(2)}) collective-permute-start(bf16[4,24,3200]{2,1,0:T(8,128)(2,1)S(1)} %pad_maximum_fusion.10), channel_id=1, source_target_pairs={{0,2},{1,3},{2,0},{3,1},{4,6},{5,7},{6,4},{7,5},{8,10},{9,11},{10,... | collective-permute-start | bytes 1843208 | tf_op jit(solution)/shard_map/ppermute | solution.py:527
  49.0 37.8 %collective-permute-start.6 = (bf16[4,24,3200]{2,1,0:T(8,128)(2,1)S(1)}, bf16[4,24,3200]{2,1,0:T(8,128)(2,1)S(1)}, u32[]{:S(2)}, u32[]{:S(2)}) collective-permute-start(bf16[4,24,3200]{2,1,0:T(8,128)(2,1)S(1)} %pad_maximum_fusion.10), channel_id=1, source_target_pairs={{0,4},{1,5},{2,6},{3,7},{4,0},{5,1},{6,2},{7,3},{8,12},{9,13},{10,... | collective-permute-start | bytes 1843208 | tf_op jit(solution)/shard_map/ppermute | solution.py:527
  52.5 34.3 %collective-permute-start.7 = (bf16[4,24,3200]{2,1,0:T(8,128)(2,1)S(1)}, bf16[4,24,3200]{2,1,0:T(8,128)(2,1)S(1)}, u32[]{:S(2)}, u32[]{:S(2)}) collective-permute-start(bf16[4,24,3200]{2,1,0:T(8,128)(2,1)S(1)} %pad_maximum_fusion.10), channel_id=1, source_target_pairs={{0,6},{1,7},{2,4},{3,5},{4,2},{5,3},{6,0},{7,1},{8,14},{9,15},{10,... | collective-permute-start | bytes 1843208 | tf_op jit(solution)/shard_map/ppermute | solution.py:527
  88.6 31.3 %collective-permute-start.14 = (bf16[4,4,24,3200]{3,2,1,0:T(8,128)(2,1)}, bf16[4,4,24,3200]{3,2,1,0:T(8,128)(2,1)}, u32[]{:S(2)}, u32[]{:S(2)}) collective-permute-start(bf16[4,4,24,3200]{3,2,1,0:T(8,128)(2,1)} %pad_maximum_fusion.1), channel_id=1, source_target_pairs={{0,1},{1,0},{2,3},{3,2},{4,5},{5,4},{6,7},{7,6},{8,9},{9,8},{10,11... | collective-permute-start | bytes 7372808 | tf_op jit(solution)/shard_map/ppermute | solution.py:527
  94.4 20.7 %collective-permute-start.16 = (bf16[64,768]{1,0:T(8,128)(2,1)S(1)}, bf16[64,768]{1,0:T(8,128)(2,1)S(1)}, u32[]{:S(2)}, u32[]{:S(2)}) collective-permute-start(bf16[64,768]{1,0:T(8,128)(2,1)S(1)} %copy-done.55), channel_id=1, source_target_pairs={{0,8},{1,9},{2,10},{3,11},{4,12},{5,13},{6,14},{7,15},{8,0},{9,1},... | collective-permute-start | bytes 294920 | tf_op jit(solution)/shard_map/ppermute | solution.py:527
  111.8 50.2 %collective-permute-start.15 = (bf16[4,128,768]{2,1,0:T(8,128)(2,1)}, bf16[4,128,768]{2,1,0:T(8,128)(2,1)}, u32[]{:S(2)}, u32[]{:S(2)}) collective-permute-start(bf16[4,128,768]{2,1,0:T(8,128)(2,1)} %pad_maximum_fusion.6.refs_8_), channel_id=1, source_target_pairs={{0,4},{1,5},{2,6},{3,7},{4,0},{5,1},{6,2},{7,3},{8,12},{9,13},{10,... | collective-permute-start | bytes 2359304 | tf_op jit(solution)/shard_map/ppermute | solution.py:527
  125.1 36.9 %collective-permute-start.19 = (bf16[4,64,768]{2,1,0:T(8,128)(2,1)}, bf16[4,64,768]{2,1,0:T(8,128)(2,1)}, u32[]{:S(2)}, u32[]{:S(2)}) collective-permute-start(bf16[4,64,768]{2,1,0:T(8,128)(2,1)} %pad_maximum_fusion.11), channel_id=1, source_target_pairs={{0,2},{1,3},{2,0},{3,1},{4,6},{5,7},{6,4},{7,5},{8,10},{9,11},{10,... | collective-permute-start | bytes 1179656 | tf_op jit(solution)/shard_map/ppermute | solution.py:527
  126.5 35.5 %collective-permute-start.20 = (bf16[4,64,768]{2,1,0:T(8,128)(2,1)}, bf16[4,64,768]{2,1,0:T(8,128)(2,1)}, u32[]{:S(2)}, u32[]{:S(2)}) collective-permute-start(bf16[4,64,768]{2,1,0:T(8,128)(2,1)} %pad_maximum_fusion.11), channel_id=1, source_target_pairs={{0,4},{1,5},{2,6},{3,7},{4,0},{5,1},{6,2},{7,3},{8,12},{9,13},{10,... | collective-permute-start | bytes 1179656 | tf_op jit(solution)/shard_map/ppermute | solution.py:527
  127.5 34.5 %collective-permute-start.21 = (bf16[4,64,768]{2,1,0:T(8,128)(2,1)}, bf16[4,64,768]{2,1,0:T(8,128)(2,1)}, u32[]{:S(2)}, u32[]{:S(2)}) collective-permute-start(bf16[4,64,768]{2,1,0:T(8,128)(2,1)} %pad_maximum_fusion.11), channel_id=1, source_target_pairs={{0,6},{1,7},{2,4},{3,5},{4,2},{5,3},{6,0},{7,1},{8,14},{9,15},{10,... | collective-permute-start | bytes 1179656 | tf_op jit(solution)/shard_map/ppermute | solution.py:527
  128.6 43.0 %all-to-all-start = ((bf16[8,128,768]{2,1,0:T(8,128)(2,1)}), bf16[8,128,768]{2,1,0:T(8,128)(2,1)}, u32[]{:S(2)}, u32[]{:S(2)}) async-start(bf16[8,128,768]{2,1,0:T(8,128)(2,1)} %bitcast.260), calls=%async_computation | async-start | bytes 3145728 | tf_op jit(solution)/shard_map/all_to_all | solution.py:608
  213.2 47.0 %all-to-all-start.1 = ((bf16[8,144,768]{2,1,0:T(8,128)(2,1)}), bf16[8,144,768]{2,1,0:T(8,128)(2,1)}, u32[]{:S(2)}, u32[]{:S(2)}) async-start(bf16[8,144,768]{2,1,0:T(8,128)(2,1)} %pad_maximum_fusion.2), calls=%async_computation.1 | async-start | bytes 3538944 | tf_op jit(solution)/shard_map/all_to_all | solution.py:608
  217.7 36.7 %collective-permute-start.25 = (bf16[4,48,4096]{2,1,0:T(8,128)(2,1)}, bf16[4,48,4096]{2,1,0:T(8,128)(2,1)}, u32[]{:S(2)}, u32[]{:S(2)}) collective-permute-start(bf16[4,48,4096]{2,1,0:T(8,128)(2,1)} %pad_maximum_fusion.3), channel_id=1, source_target_pairs={{0,4},{1,5},{2,6},{3,7},{4,0},{5,1},{6,2},{7,3},{8,12},{9,13},{10,... | collective-permute-start | bytes 4718600 | tf_op jit(solution)/shard_map/ppermute | solution.py:527
  219.5 49.7 %collective-permute-start.26 = (bf16[4,48,4096]{2,1,0:T(8,128)(2,1)}, bf16[4,48,4096]{2,1,0:T(8,128)(2,1)}, u32[]{:S(2)}, u32[]{:S(2)}) collective-permute-start(bf16[4,48,4096]{2,1,0:T(8,128)(2,1)} %pad_maximum_fusion.3), channel_id=1, source_target_pairs={{0,1},{1,0},{2,3},{3,2},{4,5},{5,4},{6,7},{7,6},{8,9},{9,8},{10,11... | collective-permute-start | bytes 4718600 | tf_op jit(solution)/shard_map/ppermute | solution.py:527
  254.4 16.9 %collective-permute-start.27 = (bf16[4,48,4096]{2,1,0:T(8,128)(2,1)}, bf16[4,48,4096]{2,1,0:T(8,128)(2,1)}, u32[]{:S(2)}, u32[]{:S(2)}) collective-permute-start(bf16[4,48,4096]{2,1,0:T(8,128)(2,1)} %collective-permute-done.25), channel_id=1, source_target_pairs={{0,1},{1,0},{2,3},{3,2},{4,5},{5,4},{6,7},{7,6},{8,9},{9,8},{10,11... | collective-permute-start | bytes 4718600 | tf_op jit(solution)/shard_map/ppermute | solution.py:527
  264.2 71.8 %collective-permute-start.37 = (bf16[256,768]{1,0:T(8,128)(2,1)}, bf16[256,768]{1,0:T(8,128)(2,1)}, u32[]{:S(2)}, u32[]{:S(2)}) collective-permute-start(bf16[256,768]{1,0:T(8,128)(2,1)} %get-tuple-element.166), channel_id=1, source_target_pairs={{0,2},{1,3},{2,0},{3,1},{4,6},{5,7},{6,4},{7,5},{8,10},{9,11},{10,... | collective-permute-start | bytes 1179656 | tf_op jit(solution)/shard_map/ppermute | solution.py:527
  267.8 86.4 %collective-permute-start.34 = (bf16[2,96,2048]{2,1,0:T(8,128)(2,1)}, bf16[2,96,2048]{2,1,0:T(8,128)(2,1)}, u32[]{:S(2)}, u32[]{:S(2)}) collective-permute-start(bf16[2,96,2048]{2,1,0:T(8,128)(2,1)} %get-tuple-element.146), channel_id=1, source_target_pairs={{0,2},{1,3},{2,0},{3,1},{4,6},{5,7},{6,4},{7,5},{8,10},{9,11},{10,... | collective-permute-start | bytes 2359304 | tf_op jit(solution)/shard_map/ppermute | solution.py:527
  269.3 84.9 %collective-permute-start.35 = (bf16[2,96,2048]{2,1,0:T(8,128)(2,1)}, bf16[2,96,2048]{2,1,0:T(8,128)(2,1)}, u32[]{:S(2)}, u32[]{:S(2)}) collective-permute-start(bf16[2,96,2048]{2,1,0:T(8,128)(2,1)} %get-tuple-element.145), channel_id=1, source_target_pairs={{0,4},{1,5},{2,6},{3,7},{4,0},{5,1},{6,2},{7,3},{8,12},{9,13},{10,... | collective-permute-start | bytes 2359304 | tf_op jit(solution)/shard_map/ppermute | solution.py:527
  271.0 83.2 %collective-permute-start.36 = (bf16[2,96,2048]{2,1,0:T(8,128)(2,1)S(1)}, bf16[2,96,2048]{2,1,0:T(8,128)(2,1)}, u32[]{:S(2)}, u32[]{:S(2)}) collective-permute-start(bf16[2,96,2048]{2,1,0:T(8,128)(2,1)S(1)} %get-tuple-element.144), channel_id=1, source_target_pairs={{0,6},{1,7},{2,4},{3,5},{4,2},{5,3},{6,0},{7,1},{8,14},{9,15},{10,... | collective-permute-start | bytes 2359304 | tf_op jit(solution)/shard_map/ppermute | solution.py:527
  329.7 49.0 %all-to-all-start.2 = ((bf16[8,144,768]{2,1,0:T(8,128)(2,1)}), bf16[8,144,768]{2,1,0:T(8,128)(2,1)}, u32[]{:S(2)}, u32[]{:S(2)}) async-start(bf16[8,144,768]{2,1,0:T(8,128)(2,1)} %get-tuple-element.93), calls=%async_computation.2 | async-start | bytes 3538944 | tf_op jit(solution)/shard_map/all_to_all | solution.py:608
  336.0 18.2 %collective-permute-start.39 = (bf16[256,768]{1,0:T(8,128)(2,1)S(1)}, bf16[256,768]{1,0:T(8,128)(2,1)}, u32[]{:S(2)}, u32[]{:S(2)}) collective-permute-start(bf16[256,768]{1,0:T(8,128)(2,1)S(1)} %get-tuple-element.164), channel_id=1, source_target_pairs={{0,6},{1,7},{2,4},{3,5},{4,2},{5,3},{6,0},{7,1},{8,14},{9,15},{10,... | collective-permute-start | bytes 1179656 | tf_op jit(solution)/shard_map/ppermute | solution.py:527
  354.2 16.5 %collective-permute-start.33 = (bf16[4,128,768]{2,1,0:T(8,128)(2,1)}, bf16[4,128,768]{2,1,0:T(8,128)(2,1)S(1)}, u32[]{:S(2)}, u32[]{:S(2)}) collective-permute-start(bf16[4,128,768]{2,1,0:T(8,128)(2,1)} %get-tuple-element.107), channel_id=1, source_target_pairs={{0,1},{1,0},{2,3},{3,2},{4,5},{5,4},{6,7},{7,6},{8,9},{9,8},{10,11... | collective-permute-start | bytes 2359304 | tf_op jit(solution)/shard_map/ppermute | solution.py:527
  354.3 20.8 %collective-permute-start.32 = (bf16[4,128,768]{2,1,0:T(8,128)(2,1)}, bf16[4,128,768]{2,1,0:T(8,128)(2,1)S(1)}, u32[]{:S(2)}, u32[]{:S(2)}) collective-permute-start(bf16[4,128,768]{2,1,0:T(8,128)(2,1)} %get-tuple-element.105), channel_id=1, source_target_pairs={{0,1},{1,0},{2,3},{3,2},{4,5},{5,4},{6,7},{7,6},{8,9},{9,8},{10,11... | collective-permute-start | bytes 2359304 | tf_op jit(solution)/shard_map/ppermute | solution.py:527
  354.8 21.8 %collective-permute-start.31 = (bf16[4,2,48,2048]{3,2,1,0:T(8,128)(2,1)}, bf16[4,2,48,2048]{3,2,1,0:T(8,128)(2,1)S(1)}, u32[]{:S(2)}, u32[]{:S(2)}) collective-permute-start(bf16[4,2,48,2048]{3,2,1,0:T(8,128)(2,1)} %get-tuple-element.103), channel_id=1, source_target_pairs={{0,1},{1,0},{2,3},{3,2},{4,5},{5,4},{6,7},{7,6},{8,9},{9,8},{10,11... | collective-permute-start | bytes 4718600 | tf_op jit(solution)/shard_map/ppermute | solution.py:527
  354.9 28.8 %collective-permute-start.30 = (bf16[4,2,48,2048]{3,2,1,0:T(8,128)(2,1)}, bf16[4,2,48,2048]{3,2,1,0:T(8,128)(2,1)}, u32[]{:S(2)}, u32[]{:S(2)}) collective-permute-start(bf16[4,2,48,2048]{3,2,1,0:T(8,128)(2,1)} %get-tuple-element.101), channel_id=1, source_target_pairs={{0,1},{1,0},{2,3},{3,2},{4,5},{5,4},{6,7},{7,6},{8,9},{9,8},{10,11... | collective-permute-start | bytes 4718600 | tf_op jit(solution)/shard_map/ppermute | solution.py:527
  357.6 110.3 %collective-permute-start.57 = (bf16[64,768]{1,0:T(8,128)(2,1)}, bf16[64,768]{1,0:T(8,128)(2,1)}, u32[]{:S(2)}, u32[]{:S(2)}) collective-permute-start(bf16[64,768]{1,0:T(8,128)(2,1)} %get-tuple-element.200), channel_id=1, source_target_pairs={{0,8},{1,9},{2,10},{3,11},{4,12},{5,13},{6,14},{7,15},{8,0},{9,1},... | collective-permute-start | bytes 294920 | tf_op jit(solution)/shard_map/ppermute | solution.py:527
  370.7 101.3 %collective-permute-start.58 = (bf16[64,768]{1,0:T(8,128)(2,1)}, bf16[64,768]{1,0:T(8,128)(2,1)}, u32[]{:S(2)}, u32[]{:S(2)}) collective-permute-start(bf16[64,768]{1,0:T(8,128)(2,1)} %get-tuple-element.199), channel_id=1, source_target_pairs={{0,16},{1,17},{2,18},{3,19},{4,20},{5,21},{6,22},{7,23},{8,24},{9,... | collective-permute-start | bytes 294920 | tf_op jit(solution)/shard_map/ppermute | solution.py:527
  375.1 96.9 %collective-permute-start.59 = (bf16[64,768]{1,0:T(8,128)(2,1)}, bf16[64,768]{1,0:T(8,128)(2,1)}, u32[]{:S(2)}, u32[]{:S(2)}) collective-permute-start(bf16[64,768]{1,0:T(8,128)(2,1)} %get-tuple-element.198), channel_id=1, source_target_pairs={{0,24},{1,25},{2,26},{3,27},{4,28},{5,29},{6,30},{7,31},{8,16},{9,... | collective-permute-start | bytes 294920 | tf_op jit(solution)/shard_map/ppermute | solution.py:527
  376.6 85.8 %collective-permute-start.65 = (bf16[4,128,768]{2,1,0:T(8,128)(2,1)}, bf16[4,128,768]{2,1,0:T(8,128)(2,1)}, u32[]{:S(2)}, u32[]{:S(2)}) collective-permute-start(bf16[4,128,768]{2,1,0:T(8,128)(2,1)} %add_convert_fusion.6), channel_id=1, source_target_pairs={{0,4},{1,5},{2,6},{3,7},{4,0},{5,1},{6,2},{7,3},{8,12},{9,13},{10,... | collective-permute-start | bytes 2359304 | tf_op jit(solution)/shard_map/ppermute | solution.py:527
  378.8 42.1 %all-to-all-start.3 = ((bf16[8,128,768]{2,1,0:T(8,128)(2,1)}), bf16[8,128,768]{2,1,0:T(8,128)(2,1)}, u32[]{:S(2)}, u32[]{:S(2)}) async-start(bf16[8,128,768]{2,1,0:T(8,128)(2,1)} %bitcast.258), calls=%async_computation.3 | async-start | bytes 3145728 | tf_op jit(solution)/shard_map/all_to_all | solution.py:608
  383.7 80.3 %collective-permute-start.60 = (bf16[4,2,48,2048]{3,2,1,0:T(8,128)(2,1)}, bf16[4,2,48,2048]{3,2,1,0:T(8,128)(2,1)}, u32[]{:S(2)}, u32[]{:S(2)}) collective-permute-start(bf16[4,2,48,2048]{3,2,1,0:T(8,128)(2,1)} %add_convert_fusion.3), channel_id=1, source_target_pairs={{0,4},{1,5},{2,6},{3,7},{4,0},{5,1},{6,2},{7,3},{8,12},{9,13},{10,... | collective-permute-start | bytes 4718600 | tf_op jit(solution)/shard_map/ppermute | solution.py:527
  463.9 16.3 %collective-permute-start.55 = (bf16[2,24,2048]{2,1,0:T(8,128)(2,1)S(1)}, bf16[2,24,2048]{2,1,0:T(8,128)(2,1)S(1)}, u32[]{:S(2)}, u32[]{:S(2)}) collective-permute-start(bf16[2,24,2048]{2,1,0:T(8,128)(2,1)S(1)} %copy-done.48), channel_id=1, source_target_pairs={{0,16},{1,17},{2,18},{3,19},{4,20},{5,21},{6,22},{7,23},{8,24},{9,... | collective-permute-start | bytes 589832 | tf_op jit(solution)/shard_map/ppermute | solution.py:527
  472.0 46.7 %collective-permute-start.66 = (bf16[128,768]{1,0:T(8,128)(2,1)}, bf16[128,768]{1,0:T(8,128)(2,1)}, u32[]{:S(2)}, u32[]{:S(2)}) collective-permute-start(bf16[128,768]{1,0:T(8,128)(2,1)} %get-tuple-element.184), channel_id=1, source_target_pairs={{0,8},{1,9},{2,10},{3,11},{4,12},{5,13},{6,14},{7,15},{8,0},{9,1},... | collective-permute-start | bytes 589832 | tf_op jit(solution)/shard_map/ppermute | solution.py:527
  472.0 50.9 %collective-permute-start.67 = (bf16[128,768]{1,0:T(8,128)(2,1)}, bf16[128,768]{1,0:T(8,128)(2,1)}, u32[]{:S(2)}, u32[]{:S(2)}) collective-permute-start(bf16[128,768]{1,0:T(8,128)(2,1)} %get-tuple-element.183), channel_id=1, source_target_pairs={{0,16},{1,17},{2,18},{3,19},{4,20},{5,21},{6,22},{7,23},{8,24},{9,... | collective-permute-start | bytes 589832 | tf_op jit(solution)/shard_map/ppermute | solution.py:527
  473.5 49.4 %collective-permute-start.68 = (bf16[128,768]{1,0:T(8,128)(2,1)}, bf16[128,768]{1,0:T(8,128)(2,1)}, u32[]{:S(2)}, u32[]{:S(2)}) collective-permute-start(bf16[128,768]{1,0:T(8,128)(2,1)} %get-tuple-element.182), channel_id=1, source_target_pairs={{0,24},{1,25},{2,26},{3,27},{4,28},{5,29},{6,30},{7,31},{8,16},{9,... | collective-permute-start | bytes 589832 | tf_op jit(solution)/shard_map/ppermute | solution.py:527
  480.2 44.5 %collective-permute-start.61 = (bf16[2,48,2048]{2,1,0:T(8,128)(2,1)}, bf16[2,48,2048]{2,1,0:T(8,128)(2,1)}, u32[]{:S(2)}, u32[]{:S(2)}) collective-permute-start(bf16[2,48,2048]{2,1,0:T(8,128)(2,1)} %get-tuple-element.161), channel_id=1, source_target_pairs={{0,8},{1,9},{2,10},{3,11},{4,12},{5,13},{6,14},{7,15},{8,0},{9,1},... | collective-permute-start | bytes 1179656 | tf_op jit(solution)/shard_map/ppermute | solution.py:527
  481.1 43.7 %collective-permute-start.62 = (bf16[2,48,2048]{2,1,0:T(8,128)(2,1)S(1)}, bf16[2,48,2048]{2,1,0:T(8,128)(2,1)}, u32[]{:S(2)}, u32[]{:S(2)}) collective-permute-start(bf16[2,48,2048]{2,1,0:T(8,128)(2,1)S(1)} %get-tuple-element.160), channel_id=1, source_target_pairs={{0,16},{1,17},{2,18},{3,19},{4,20},{5,21},{6,22},{7,23},{8,24},{9,... | collective-permute-start | bytes 1179656 | tf_op jit(solution)/shard_map/ppermute | solution.py:527
  495.0 23.6 %all-to-all-start.4 = ((f32[32,1,240]{2,1,0:T(1,128)}), f32[32,1,240]{2,1,0:T(1,128)S(1)}, u32[]{:S(2)}, u32[]{:S(2)}) async-start(f32[32,1,240]{2,1,0:T(1,128)} %copy.102), calls=%async_computation.4 | async-start | bytes 65536 | tf_op jit(solution)/shard_map/all_to_all | solution.py:801
  522.9 35.5 %collective-permute-start.40 = (bf16[4,3,96,768]{3,2,1,0:T(8,128)(2,1)}, bf16[4,3,96,768]{3,2,1,0:T(8,128)(2,1)S(1)}, u32[]{:S(2)}, u32[]{:S(2)}) collective-permute-start(bf16[4,3,96,768]{3,2,1,0:T(8,128)(2,1)} %get-tuple-element.121), channel_id=1, source_target_pairs={{0,1},{1,0},{2,3},{3,2},{4,5},{5,4},{6,7},{7,6},{8,9},{9,8},{10,11... | collective-permute-start | bytes 5308424 | tf_op jit(solution)/shard_map/ppermute | solution.py:527
  532.9 29.6 %collective-permute-start.64 = (bf16[2,2,48,2048]{3,2,1,0:T(8,128)(2,1)S(1)}, bf16[2,2,48,2048]{3,2,1,0:T(8,128)(2,1)S(1)}, u32[]{:S(2)}, u32[]{:S(2)}) collective-permute-start(bf16[2,2,48,2048]{3,2,1,0:T(8,128)(2,1)S(1)} %pad_maximum_fusion.8), channel_id=1, source_target_pairs={{0,1},{1,0},{2,3},{3,2},{4,5},{5,4},{6,7},{7,6},{8,9},{9,8},{10,11... | collective-permute-start | bytes 2359304 | tf_op jit(solution)/shard_map/ppermute | solution.py:527
  560.5 19.5 %collective-permute-start.42 = (bf16[3,96,768]{2,1,0:T(8,128)(2,1)S(1)}, bf16[3,96,768]{2,1,0:T(8,128)(2,1)S(1)}, u32[]{:S(2)}, u32[]{:S(2)}) collective-permute-start(bf16[3,96,768]{2,1,0:T(8,128)(2,1)S(1)} %get-tuple-element.151), channel_id=1, source_target_pairs={{0,4},{1,5},{2,6},{3,7},{4,0},{5,1},{6,2},{7,3},{8,12},{9,13},{10,... | collective-permute-start | bytes 1327112 | tf_op jit(solution)/shard_map/ppermute | solution.py:527
  561.0 19.1 %collective-permute-start.43 = (bf16[3,96,768]{2,1,0:T(8,128)(2,1)S(1)}, bf16[3,96,768]{2,1,0:T(8,128)(2,1)S(1)}, u32[]{:S(2)}, u32[]{:S(2)}) collective-permute-start(bf16[3,96,768]{2,1,0:T(8,128)(2,1)S(1)} %get-tuple-element.150), channel_id=1, source_target_pairs={{0,6},{1,7},{2,4},{3,5},{4,2},{5,3},{6,0},{7,1},{8,14},{9,15},{10,... | collective-permute-start | bytes 1327112 | tf_op jit(solution)/shard_map/ppermute | solution.py:527
  (116 other events, 893.8 us)
Sparse Core Ops, SparseCore 0:
  17.4 99.2 all-gather.1
